TPU v7x, 32 devices: a whole 2x2x4 slice. The times are simulated.
32 devices in a mesh: groups: 2 (over y), dap: 4 (over z), sub: 4 (over x, core).
Axes of the slice: x: 2, y: 2, z: 4, core: 2. Of those that a mesh axis runs over, the one named last changes fastest.
Arguments:
- pair: bfloat16 [128, 64, 128], P(('groups', 'dap', 'sub')), parts along dimension 0, may hold values from -6 to 6
- cotangent: bfloat16 [128, 64, 128], P(('groups', 'dap', 'sub')), parts along dimension 0, may hold values from -6 to 6
- residue_mask: int32 [128], P('groups'), parts along dimension 0, may hold values 0 or 1
- chain_labels: int32 [128], P('groups'), parts along dimension 0, may hold values from 0 to 3, never falling along the last dimension, each value on 1 to 32 neighbouring positions
- gain: float32 [128], replicated, may hold values from 0.5 to 1.5
- projection_weight: bfloat16 [4, 128, 128], replicated, may hold values from -0.5 to 0.5
- bias_weight: bfloat16 [128, 4], replicated, may hold values from -0.5 to 0.5
- output_weight: bfloat16 [128, 128], replicated, may hold values from -0.5 to 0.5
- position_bias_table: float32 [4, 66], replicated, may hold values from -4 to 240
- adapter_down_maps: bfloat16 [4, 128, 16], replicated, may hold values from -0.5 to 0.5
- adapter_up_maps: bfloat16 [4, 16, 128], replicated, may hold values from -1.5 to 1.5
Outputs:
- pair_grad: bfloat16 [128, 64, 128], P(('groups', 'dap', 'sub')), parts along dimension 0
- down_grad: float32 [8, 128, 16], P('groups'), parts along dimension 0
- up_grad: float32 [8, 16, 128], P('groups'), parts along dimension 0
There are 2 independent parts, one for each index of `groups`. A program takes and returns all parts, laid end to end along the dimension named above; an argument that names none is the same for every part. Nothing has to cross between parts.
All inputs are finite; a program needn't handle non-finite values.
Results may differ from a plain program's by a relative error of at most 0.015.
The roundings to bfloat16 on the way count: a program that leaves them out, or rounds other values in their place, can miss the bound.
Values may be sent and summed in bfloat16 or wider, within the bound.
No kernel may reach another device: no remote copies, remote signals or barrier semaphores. Data moves between devices by JAX's collectives and lax.ppermute only.
A program may use at most 64 MiB of HBM per device.

v0:
```python
import math

import jax
import jax.numpy as jnp
from jax import lax
from jax.sharding import PartitionSpec as P

epsilon = 1e-05


def normalize(pair_rows, gain):
    widened = pair_rows.astype(jnp.float32)
    average = jnp.mean(widened, axis=-1, keepdims=True)
    centred = widened - average
    spread = jnp.mean(centred * centred, axis=-1, keepdims=True)
    return centred * lax.rsqrt(spread + epsilon) * gain


def relative_bias(chain_labels, row_start, row_count, position_bias_table):
    key_count = chain_labels.shape[0]
    bin_count = position_bias_table.shape[1]
    reach_max = (bin_count - 2) // 2
    query_pos = row_start + jnp.arange(row_count, dtype=jnp.int32)
    key_pos = jnp.arange(key_count, dtype=jnp.int32)
    query_chain = lax.dynamic_slice_in_dim(chain_labels, row_start, row_count)
    same_chain = query_chain[:, None] == chain_labels[None, :]
    offset = jnp.clip(key_pos[None, :] - query_pos[:, None], -reach_max, reach_max) + reach_max
    bin_index = jnp.where(same_chain, offset, bin_count - 1)
    onehot = (
        bin_index[:, :, None] == jnp.arange(bin_count, dtype=jnp.int32)[None, None, :]
    ).astype(jnp.float32)
    return jnp.einsum("rkb,hb->hrk", onehot, position_bias_table, precision=lax.Precision.HIGHEST)


def row_attention(
    layer_normed_row,
    complete_bias,
    key_valid_mask,
    projection_weight,
    output_weight,
    adapter_down_maps,
    adapter_up_maps,
):
    key_count, channel_count = layer_normed_row.shape
    head_count = complete_bias.shape[0]
    head_width = channel_count // head_count
    score_scale = 1.0 / math.sqrt(head_width)

    def adapted(projection_index):
        frozen_term = jnp.dot(
            layer_normed_row.astype(jnp.bfloat16),
            projection_weight[projection_index],
            preferred_element_type=jnp.float32,
        )
        reduced_update = jnp.dot(
            layer_normed_row.astype(jnp.bfloat16),
            adapter_down_maps[projection_index].astype(jnp.bfloat16),
            preferred_element_type=jnp.float32,
        ).astype(jnp.bfloat16)
        return frozen_term + jnp.dot(
            reduced_update,
            adapter_up_maps[projection_index].astype(jnp.bfloat16),
            preferred_element_type=jnp.float32,
        )

    queries = adapted(0).astype(jnp.bfloat16).reshape(key_count, head_count, head_width)
    keys_all = adapted(1).astype(jnp.bfloat16).reshape(key_count, head_count, head_width)
    values_all = adapted(2).astype(jnp.bfloat16).reshape(key_count, head_count, head_width)
    scores = (
        jnp.einsum("jhd,khd->hjk", queries, keys_all, preferred_element_type=jnp.float32)
        * score_scale
        + complete_bias
    )
    scores = jnp.where(key_valid_mask[None, None, :], scores, -1000000000.0)
    weights = jax.nn.softmax(scores, axis=-1).astype(jnp.bfloat16)
    attended = jnp.einsum(
        "hjk,khd->jhd", weights, values_all, preferred_element_type=jnp.float32
    ).reshape(key_count, channel_count)
    gating = jax.nn.sigmoid(
        jnp.dot(
            layer_normed_row.astype(jnp.bfloat16),
            projection_weight[3],
            preferred_element_type=jnp.float32,
        )
    )
    gated_output = (gating * attended).astype(jnp.bfloat16)
    reduced_output = jnp.dot(
        gated_output, adapter_down_maps[3].astype(jnp.bfloat16), preferred_element_type=jnp.float32
    ).astype(jnp.bfloat16)
    return jnp.dot(gated_output, output_weight, preferred_element_type=jnp.float32) + jnp.dot(
        reduced_output, adapter_up_maps[3].astype(jnp.bfloat16), preferred_element_type=jnp.float32
    )


def local(
    pair,
    cotangent,
    residue_mask,
    chain_labels,
    gain,
    projection_weight,
    bias_weight,
    output_weight,
    position_bias_table,
    adapter_down_maps,
    adapter_up_maps,
):
    local_rows = pair.shape[0]
    moved_pair, moved_cot = (
        lax.all_to_all(pair, ("dap", "sub"), split_axis=1, concat_axis=0, tiled=True),
        lax.all_to_all(cotangent, ("dap", "sub"), split_axis=1, concat_axis=0, tiled=True),
    )
    columns_in = jnp.transpose(moved_pair, (1, 0, 2))
    upstream = jnp.transpose(moved_cot, (1, 0, 2))
    key_valid_mask = residue_mask > 0
    row_start = lax.axis_index(("dap", "sub")) * local_rows
    rel_bias = relative_bias(chain_labels, row_start, local_rows, position_bias_table)
    normed, norm_pull = jax.vjp(lambda values: normalize(values, gain), columns_in)

    def bias_rows_of(normed_rows):
        projected = jnp.einsum(
            "rkc,ch->hrk",
            normed_rows.astype(jnp.bfloat16),
            bias_weight,
            preferred_element_type=jnp.float32,
        )
        return (projected + rel_bias).astype(jnp.bfloat16)

    own_bias, bias_pull = jax.vjp(bias_rows_of, normed)
    complete_bias = lax.all_gather(own_bias, ("dap", "sub"), axis=1, tiled=True).astype(jnp.float32)
    down_matrix = adapter_down_maps.astype(jnp.float32)
    up_matrix = adapter_up_maps.astype(jnp.float32)

    def per_row(carry, item):
        layer_normed_row, upstream_row = item

        def local_attend(row_values, bias_values, down_values, up_values):
            return row_attention(
                row_values,
                bias_values,
                key_valid_mask,
                projection_weight,
                output_weight,
                down_values,
                up_values,
            )

        unused_value, row_pull = jax.vjp(
            local_attend, layer_normed_row, complete_bias, down_matrix, up_matrix
        )
        grad_row, grad_bias, grad_down, grad_up = row_pull(upstream_row.astype(jnp.float32))
        return ((carry[0] + grad_bias, carry[1] + grad_down, carry[2] + grad_up), grad_row)

    initial = (
        jnp.zeros_like(complete_bias),
        jnp.zeros_like(down_matrix),
        jnp.zeros_like(up_matrix),
    )
    (bias_grad, down_part, up_part), grad_rows = lax.scan(per_row, initial, (normed, upstream))
    whole_grad = lax.psum(bias_grad, ("dap", "sub"))
    own_grad = lax.dynamic_slice_in_dim(whole_grad, row_start, local_rows, 1)
    down_grad, up_grad = lax.psum((down_part, up_part), ("dap", "sub"))
    grad_normed = grad_rows + bias_pull(own_grad.astype(jnp.bfloat16))[0]
    grad_columns = norm_pull(grad_normed)[0]
    pair_grad = lax.all_to_all(
        jnp.transpose(grad_columns, (1, 0, 2)),
        ("dap", "sub"),
        split_axis=0,
        concat_axis=1,
        tiled=True,
    )
    return (pair_grad, down_grad, up_grad)


def solution(mesh):
    return jax.shard_map(
        local,
        mesh=mesh,
        in_specs=(
            P(("groups", "dap", "sub"), None, None),
            P(("groups", "dap", "sub"), None, None),
            P("groups"),
            P("groups"),
            P(),
            P(),
            P(),
            P(),
            P(),
            P(),
            P(),
        ),
        out_specs=(
            P(("groups", "dap", "sub"), None, None),
            P("groups", None, None),
            P("groups", None, None),
        ),
        check_vma=False,
    )
```

profile of v0, /device:TPU:0, one launch (start us, length us, event | category | flops | bytes accessed | tf_op | source)
XLA Modules:
  0.0 142.8 jit_solution(14055502664169965205)
XLA Ops:
  0.6 1.5 %copy.56 = bf16[4,64,128]{2,0,1:T(4,128)(2,1)} copy(bf16[4,64,128]{2,1,0:T(8,128)(2,1)} %param.13) | data formatting | bytes 131072 | tf_op args[0]
  2.2 7.5 %all-to-all-start = ((bf16[4,64,128]{2,0,1:T(4,128)(2,1)}), bf16[4,64,128]{2,0,1:T(4,128)(2,1)S(1)}, u32[]{:S(2)}, u32[]{:S(2)}) async-start(bf16[4,64,128]{2,0,1:T(4,128)(2,1)} %copy.56), calls=%async_computation | async-start | bytes 131072 | tf_op jit(solution)/shard_map/all_to_all | solution.py:110
  9.8 0.7 copy-done.3
  10.5 0.7 copy.58
  11.2 0.7 copy-done.8
  12.0 0.3 fusion.90
  12.3 0.3 copy-done.9
  12.7 3.9 %all-to-all-done = bf16[4,64,128]{2,0,1:T(4,128)(2,1)S(1)} async-done(((bf16[4,64,128]{2,0,1:T(4,128)(2,1)}), bf16[4,64,128]{2,0,1:T(4,128)(2,1)S(1)}, u32[]{:S(2)}, u32[]{:S(2)}) %all-to-all-start) | async-done | bytes 65568 | tf_op jit(solution)/shard_map/all_to_all | solution.py:110
  16.6 3.5 %all-to-all-start.1 = ((bf16[4,64,128]{2,0,1:T(4,128)(2,1)}), bf16[4,64,128]{2,0,1:T(4,128)(2,1)S(1)}, u32[]{:S(2)}, u32[]{:S(2)}) async-start(bf16[4,64,128]{2,0,1:T(4,128)(2,1)} %copy.58), calls=%async_computation.1 | async-start | bytes 131072 | tf_op jit(solution)/shard_map/all_to_all | solution.py:111
  20.4 0.6 copy-done.7
  21.2 0.5 copy-done.6
  21.9 21.8 %all_gather.3 = bf16[4,64,64]{2,0,1:T(4,128)(2,1)S(1)} all-gather(bf16[4,4,64]{2,0,1:T(4,128)(2,1)S(1)} %fusion.89), channel_id=1, replica_groups=mesh['groups'=2,'dap'=4,'sub'=4] {'dap','sub'}, dimensions={1}, use_global_device_ids=true | all-gather | bytes 34816 | tf_op jit(solution)/shard_map/all_gather | solution.py:130
  43.9 0.7 copy-done.1
  44.7 27.4 %while.19 = (s32[]{:T(128)}, f32[4,64,64]{1,2,0:T(8,128)S(1)}, f32[4,128,16]{1,2,0:T(8,128)S(1)}, f32[4,16,128]{2,1,0:T(8,128)S(1)}, f32[4,64,128]{2,1,0:T(8,128...) while((s32[]{:T(128)}, f32[4,64,64]{1,2,0:T(8,128)S(1)}, ...), condition=%wide.region_6.7_spmd.clone, body=%wide.region_2.6_spmd.clone.sunk | while | flops 32097472 | bytes 3474837 | solution.py:159
  45.6 0.2 fusion.347
  46.1 0.2 fusion.341
  46.5 0.2 fusion.339
  47.1 0.2 fusion.342
  47.4 0.2 fusion.343
  48.4 0.2 fusion.356
  49.3 0.2 multiply_reduce_fusion.4
  52.5 0.2 fusion.347
  53.0 0.2 fusion.341
  53.4 0.2 fusion.339
  54.0 0.2 fusion.342
  54.2 0.2 fusion.343
  55.3 0.2 fusion.356
  56.2 0.2 multiply_reduce_fusion.4
  59.4 0.2 fusion.347
  59.8 0.2 fusion.341
  60.3 0.2 fusion.339
  60.9 0.2 fusion.342
  61.1 0.2 fusion.343
  62.1 0.2 fusion.356
  63.0 0.2 multiply_reduce_fusion.4
  66.2 0.2 fusion.347
  66.7 0.2 fusion.341
  67.1 0.2 fusion.339
  67.7 0.2 fusion.342
  67.9 0.2 fusion.343
  69.0 0.2 fusion.356
  69.9 0.2 multiply_reduce_fusion.4
  72.2 59.6 %all-reduce.10 = (bf16[4,64,64]{2,0,1:T(4,128)(2,1)S(1)}, f32[4,128,16]{1,2,0:T(8,128)}, f32[4,16,128]{2,1,0:T(8,128)}) all-reduce(f32[4,64,64]{2,0,1:T(4,128)S(1)} %copy.61, f32[4,128,16]{1,2,0:T(8,128)S(1)} %get-tuple-element.219, f32[4,16,128]{2,1,0:T(8,128)S(1)} %get-tuple-element.220), channel_id=1, replica_groups=mesh['groups'=2,'dap'=4,'sub'=4] {'dap','sub'}, use_global_device_ids=true, to_apply=%region_7.8 | all-reduce | flops 32768 | bytes 229376 | tf_op jit(solution)/shard_map/psum | solution.py:160
  131.8 0.3 multiply_reduce_fusion.1
  132.1 0.3 fusion.94
  132.4 0.2 fusion.91
  132.7 9.5 %all_to_all.45 = bf16[64,4,128]{2,1,0:T(4,128)(2,1)S(1)} all-to-all(bf16[64,4,128]{2,1,0:T(4,128)(2,1)S(1)} %copy.62), channel_id=1, replica_groups=mesh['groups'=2,'dap'=4,'sub'=4] {'dap','sub'}, dimensions={0} | all-to-all | bytes 131072 | tf_op jit(solution)/shard_map/all_to_all | solution.py:165
  142.1 0.7 copy.63
  (210 shorter events, 22.4 us)
Async XLA Ops:
  0.6 11.4 %copy-start = (f32[4,66]{1,0:T(4,128)S(1)}, f32[4,66]{1,0:T(4,128)}, u32[]{:S(2)}) copy-start(f32[4,66]{1,0:T(4,128)} %param.21) | copy-start | bytes 3172
  2.2 7.6 %copy-start.4 = (bf16[4,128,16]{1,2,0:T(8,128)(2,1)S(1)}, bf16[4,128,16]{1,2,0:T(8,128)(2,1)}, u32[]{:S(2)}) copy-start(bf16[4,128,16]{1,2,0:T(8,128)(2,1)} %param.22) | copy-start | bytes 49156
  2.2 7.6 %copy-start.5 = (bf16[4,16,128]{2,1,0:T(8,128)(2,1)S(1)}, bf16[4,16,128]{2,1,0:T(8,128)(2,1)}, u32[]{:S(2)}) copy-start(bf16[4,16,128]{2,1,0:T(8,128)(2,1)} %param.23) | copy-start | bytes 49156
  2.2 14.4 %all-to-all-start = ((bf16[4,64,128]{2,0,1:T(4,128)(2,1)}), bf16[4,64,128]{2,0,1:T(4,128)(2,1)S(1)}, u32[]{:S(2)}, u32[]{:S(2)}) async-start(bf16[4,64,128]{2,0,1:T(4,128)(2,1)} %copy.56), calls=%async_computation | async-start | bytes 131072 | tf_op jit(solution)/shard_map/all_to_all | solution.py:110
  9.7 0.8 copy-start.3
  11.2 0.7 copy-start.8
  12.0 0.7 copy-start.9
  16.6 27.3 %all-to-all-start.1 = ((bf16[4,64,128]{2,0,1:T(4,128)(2,1)}), bf16[4,64,128]{2,0,1:T(4,128)(2,1)S(1)}, u32[]{:S(2)}, u32[]{:S(2)}) async-start(bf16[4,64,128]{2,0,1:T(4,128)(2,1)} %copy.58), calls=%async_computation.1 | async-start | bytes 131072 | tf_op jit(solution)/shard_map/all_to_all | solution.py:111
  20.4 0.7 copy-start.7
  21.1 0.7 copy-start.6
  43.7 0.9 copy-start.1
  43.9 0.8 copy-start.2
where the time goes:
time: 143 us
  blocking collectives  90.9 us (64%)
  matrix products  24.1 us (17%)
  starting transfers between devices  11 us (8%)
  local copies, waits for them, and re-layouts  9.26 us (6%)
  waiting for transfers between devices  3.91 us (3%)
  other arithmetic  2.39 us (2%)
    psum x1, blocking collectives, local(): whole_grad = lax.psum(bias_grad, ('dap', 'sub'))  59.6 us
    all_gather x1, blocking collectives, local(): lax.all_gather(own_bias, ('dap', 'sub'), axis=1, tiled=True)  21.8 us
    all_to_all x1, blocking collectives, local(): lax.all_to_all(jnp.transpose(grad_columns, (1, 0, 2)), ('dap', 'sub'), sp...  9.48 us
    all_to_all x1, starting transfers between devices, local(): lax.all_to_all(pair, ('dap', 'sub'), split_axis=1, concat_axis=0, tiled=T...  7.49 us
    unnamed x23, local copies, waits for them, and re-layouts  5.99 us
    dot_general x36, matrix products, adapted(): jnp.dot(reduced_update, adapter_up_maps[projection_index].astype(jnp.bflo...  5.44 us
    dot_general x36, matrix products, adapted(): jnp.dot(layer_normed_row.astype(jnp.bfloat16), adapter_down_maps[projecti...  5.25 us
    all_to_all x1, waiting for transfers between devices, local(): lax.all_to_all(pair, ('dap', 'sub'), split_axis=1, concat_axis=0, tiled=T...  3.91 us
  transfers between devices with their start and end apart: 2, of which 1 were waited for; matrix products, arithmetic and copies ran while one was open for 1% of the time, Pallas kernels for 0%

commit v1 on v0

v1 whole, which is shorter than its diff:
```python
import functools
import math

import jax
import jax.numpy as jnp
from jax import lax
from jax.experimental import pallas as pl
from jax.experimental.pallas import tpu as pltpu
from jax.sharding import PartitionSpec as P

epsilon = 1e-05
lanes = 128
block = 256
masked_bias = -3e38
group_axes = ("dap", "sub")
vmem = pl.BlockSpec(memory_space=pltpu.VMEM)
smem = pl.BlockSpec(memory_space=pltpu.SMEM)


def nn(left, right):
    return jnp.dot(left, right, preferred_element_type=jnp.float32)


def nt(left, right):
    return lax.dot_general(left, right, (((1,), (1,)), ((), ())), preferred_element_type=jnp.float32)


def tn(left, right):
    return lax.dot_general(left, right, (((0,), (0,)), ((), ())), preferred_element_type=jnp.float32)


def half(values):
    return values.astype(jnp.bfloat16)


def repeat(count, body):
    if count == 1:
        body(0)
    else:
        lax.fori_loop(0, count, lambda step, carry: (body(step), carry)[1], 0)


def before_kernel(
    mask_ref, label_ref, label_row_ref, pair_ref, cot_ref, gain_ref, bias_weight_ref, table_ref,
    send_ref, unit_ref, inverse_ref, normed_ref, cells_ref, bias_ref,
):
    own, count, channels = pair_ref.shape
    peers = count // own
    heads, bins = table_ref.shape
    reach = (bins - 2) // 2
    first = lax.axis_index(group_axes) * own
    bias_rows = heads * count // lanes
    gain = gain_ref[...]
    key_pos = lax.broadcasted_iota(jnp.int32, (1, count), 1)
    bin_ids = lax.broadcasted_iota(jnp.int32, (bins, count), 0)
    for row in range(own):
        here = first + row
        values = pair_ref[row].astype(jnp.float32)
        centred = values - jnp.mean(values, axis=-1, keepdims=True)
        inverse = lax.rsqrt(jnp.mean(centred * centred, axis=-1, keepdims=True) + epsilon)
        unit = centred * inverse
        normed = unit * gain
        unit_ref[row * count : (row + 1) * count] = unit
        inverse_ref[row * count : (row + 1) * count] = inverse
        normed_ref[row * count : (row + 1) * count] = normed
        same = label_row_ref[...] == label_ref[here]
        offset = jnp.clip(here - key_pos, -reach, reach) + reach
        onehot = (bin_ids == jnp.where(same, offset, bins - 1)).astype(jnp.float32)
        relative = lax.dot_general(
            table_ref[...], onehot, (((1,), (0,)), ((), ())),
            precision=lax.Precision.HIGHEST, preferred_element_type=jnp.float32,
        )
        bias = half(nt(bias_weight_ref[...], half(normed)) + relative).astype(jnp.float32)
        bias = jnp.where(mask_ref[here] > 0, bias, masked_bias)
        for head in range(heads):
            if count < lanes:
                each = lanes // count
                place = (head % each) * count
                bias_ref[row * bias_rows + head // each, place : place + count] = bias[head]
            else:
                for part in range(count // lanes):
                    bias_ref[row * bias_rows + head * (count // lanes) + part, :] = bias[
                        head, part * lanes : (part + 1) * lanes
                    ]
    cell_rows = own * own

    def scatter():
        for row in range(own):
            for place in range(own):
                cells_ref[pl.ds(row * own + place, peers, stride=cell_rows)] = normed_ref[
                    pl.ds(row * count + place, peers, stride=own)
                ]
        return half(cells_ref[...]).reshape(peers, cell_rows, channels)

    send_ref[:, 0:cell_rows] = scatter()
    for row in range(own):
        normed_ref[row * count : (row + 1) * count] = cot_ref[row].astype(jnp.float32)
    send_ref[:, cell_rows : 2 * cell_rows] = scatter()
    bias_all = half(bias_ref[...])
    send_ref[:, 2 * cell_rows :] = jnp.broadcast_to(bias_all[None], (peers, *bias_all.shape))


def middle_kernel(
    recv_ref, weight_ref, out_weight_ref, down_ref, up_ref,
    send_ref,
    rows_ref, x_ref, u_ref, bias_ref, q_ref, k_ref, v_ref, da_ref, gate_ref, dgated_ref,
    att_ref, dq_ref, dk_ref, dv_ref, bias_grad_ref, adapter_ref,
    *, own, heads, sent,
):
    peers = recv_ref.shape[0]
    channels = recv_ref.shape[2]
    count = own * peers
    cell_rows = own * own
    width = channels // heads
    scale = 1.0 / math.sqrt(width)
    rank = down_ref.shape[1]
    bias_rows = heads * count // lanes
    total = own * count
    joint = min(count, block)
    joint_heads = block // joint

    for target, offset in ((x_ref, 0), (u_ref, cell_rows)):
        rows_ref[...] = recv_ref[:, offset : offset + cell_rows].astype(jnp.float32).reshape(total, channels)
        for place in range(own):
            target[place * count : (place + 1) * count] = half(rows_ref[pl.ds(place, count, stride=own)])
    gathered = recv_ref[:, 2 * cell_rows :].astype(jnp.float32)
    bias_grad_ref[...] = gathered.reshape(count * bias_rows, lanes)
    for part in range(bias_rows):
        bias_ref[:, part * lanes : (part + 1) * lanes] = bias_grad_ref[pl.ds(part, count, stride=bias_rows)]

    weights = [weight_ref[index] for index in range(4)]
    downs = [down_ref[index] for index in range(4)]
    ups = [up_ref[index] for index in range(4)]

    def project(step):
        rows = pl.ds(pl.multiple_of(step * block, block), block)
        x = x_ref[rows]
        u = u_ref[rows]
        for index, target in enumerate((q_ref, k_ref, v_ref)):
            low = half(nt(x, downs[index]))
            target[rows] = half(nn(x, weights[index]) + nn(low, ups[index]))
        gate = jax.nn.sigmoid(nn(x, weights[3]))
        dgated = half(nt(u, out_weight_ref[...]) + nn(half(nt(u, ups[3])), downs[3])).astype(jnp.float32)
        gate_ref[rows] = gate
        dgated_ref[rows] = dgated
        da_ref[rows] = half(dgated * gate)

    repeat(total // block, project)

    head_of = lax.broadcasted_iota(jnp.int32, (1, channels), 1) // width
    blocks = heads * count // block

    def attend(row, part):
        start = part * block // count
        column = pl.multiple_of(part * block, block)
        first = 0 if count <= block else pl.multiple_of(lax.rem(part * block, count), block)
        queries = pl.ds(row * count + first, joint)
        keys = pl.ds(row * count, count)
        spots = [(head_of == start + head).astype(jnp.float32) for head in range(joint_heads)]

        def spread(values):
            return jnp.concatenate([values * half(spot) for spot in spots], axis=0)

        def collect(values):
            return sum(values[head * joint : (head + 1) * joint] * spots[head] for head in range(joint_heads))

        q_wide = spread(q_ref[queries])
        da_wide = spread(da_ref[queries])
        k_all = k_ref[keys]
        v_all = v_ref[keys]
        bias = bias_ref[:, pl.ds(column, block)]
        valid = bias > -1e38
        scores = jnp.where(valid, nt(k_all, q_wide) * scale + bias, -1000000000.0)
        powers = jnp.exp(scores - jnp.max(scores, axis=0, keepdims=True))
        chances = powers / jnp.sum(powers, axis=0, keepdims=True)
        rounded = half(chances)
        dchances = half(nt(v_all, da_wide)).astype(jnp.float32)
        inner = dchances * chances
        dscores = inner - chances * jnp.sum(inner, axis=0, keepdims=True)
        dscores = jnp.where(valid, dscores, 0.0)
        scaled = half(dscores * scale)
        return (
            queries, keys, column,
            collect(tn(rounded, v_all)), collect(tn(scaled, k_all)),
            nn(scaled, q_wide), nn(rounded, da_wide), dscores,
        )

    if blocks == 1:
        bias_grad = None
        for row in range(own):
            queries, keys, column, att, dq, dk, dv, dscores = attend(row, 0)
            att_ref[queries] = att
            dq_ref[queries] = dq
            dk_ref[keys] = dk
            dv_ref[keys] = dv
            bias_grad = dscores if bias_grad is None else bias_grad + dscores
        bias_ref[...] = bias_grad
    else:
        bias_sum_ref = bias_grad_ref
        for ref in (att_ref, dq_ref, dk_ref, dv_ref):
            ref[...] = jnp.zeros_like(ref)

        def each(part):
            def each_row(row, bias_grad):
                queries, keys, column, att, dq, dk, dv, dscores = attend(row, part)
                att_ref[queries] += att
                dq_ref[queries] += dq
                dk_ref[keys] += dk
                dv_ref[keys] += dv
                return bias_grad + dscores

            bias_grad = lax.fori_loop(0, own, each_row, jnp.zeros((count, block), jnp.float32))
            bias_ref[:, pl.ds(pl.multiple_of(part * block, block), block)] = bias_grad

        repeat(blocks, each)
    for part in range(bias_rows):
        bias_grad_ref[pl.ds(part, count, stride=bias_rows)] = bias_ref[:, part * lanes : (part + 1) * lanes]

    adapter_ref[...] = jnp.zeros_like(adapter_ref)

    def finish(step):
        rows = pl.ds(pl.multiple_of(step * block, block), block)
        x = x_ref[rows]
        u = u_ref[rows]
        att = att_ref[rows]
        gate = gate_ref[rows]
        dgated = dgated_ref[rows]
        gated = half(gate * att)
        dgate = half(dgated * att * (gate * (1.0 - gate)))
        low_out = half(nt(downs[3], gated))
        dlow_out = half(nt(ups[3], u))
        downs_grad = [None] * 3 + [nn(dlow_out, gated)]
        ups_grad = [None] * 3 + [nn(low_out, u)]
        grad = nt(dgate, weights[3])
        for index, source in enumerate((dq_ref, dk_ref, dv_ref)):
            dproj = half(source[rows])
            ups_grad[index] = nn(half(nt(downs[index], x)), dproj)
            downs_grad[index] = nn(half(nt(ups[index], dproj)), x)
            grad = grad + nt(dproj, weights[index]) + nn(half(nt(dproj, ups[index])), downs[index])
        for index in range(4):
            adapter_ref[index * rank : (index + 1) * rank] += downs_grad[index]
            adapter_ref[(4 + index) * rank : (5 + index) * rank] += ups_grad[index]
        rows_ref[rows] = grad

    repeat(total // block, finish)

    for row in range(own):
        for place in range(own):
            send_ref[pl.ds(row * own + place, peers, stride=sent)] = rows_ref[
                pl.ds(place * count + row, peers, stride=own)
            ]
    bias_chunk = own * bias_rows
    adapter_chunk = adapter_ref.shape[0] // peers
    for peer in range(peers):
        base = peer * sent + cell_rows
        send_ref[base : base + bias_chunk] = bias_grad_ref[peer * bias_chunk : (peer + 1) * bias_chunk]
        base = base + bias_chunk
        send_ref[base : base + adapter_chunk] = adapter_ref[peer * adapter_chunk : (peer + 1) * adapter_chunk]


def adapter_kernel(recv_ref, send_ref, *, offset):
    peers = recv_ref.shape[0]
    chunk = send_ref.shape[1]
    send_ref[...] = jnp.broadcast_to(
        jnp.sum(recv_ref[:, offset : offset + chunk], axis=0, keepdims=True), send_ref.shape
    )


def after_kernel(
    recv_ref, unit_ref, inverse_ref, gain_ref, bias_weight_ref, out_ref, rows_ref, bias_ref, *, sent
):
    own, count, channels = out_ref.shape
    peers = count // own
    heads = bias_weight_ref.shape[0]
    cell_rows = own * own
    bias_rows = heads * count // lanes
    for row in range(own):
        for place in range(own):
            rows_ref[pl.ds(row * count + place, peers, stride=own)] = recv_ref[
                pl.ds(row * own + place, peers, stride=sent)
            ]
    summed = recv_ref[cell_rows : cell_rows + own * bias_rows]
    for peer in range(1, peers):
        base = peer * sent + cell_rows
        summed = summed + recv_ref[base : base + own * bias_rows]
    bias_ref[...] = summed
    for row in range(own):
        pieces = []
        for head in range(heads):
            if count < lanes:
                each = lanes // count
                place = (head % each) * count
                line = row * bias_rows + head // each
                pieces.append(bias_ref[line : line + 1, place : place + count])
            else:
                parts = count // lanes
                line = row * bias_rows + head * parts
                pieces.append(
                    jnp.concatenate([bias_ref[line + part : line + part + 1] for part in range(parts)], axis=1)
                )
        bias_grad = half(jnp.concatenate(pieces, axis=0))
        rows = slice(row * count, (row + 1) * count)
        unit = unit_ref[rows]
        grad = (rows_ref[rows] + tn(bias_grad, bias_weight_ref[...])) * gain_ref[...]
        along = jnp.mean(grad * unit, axis=-1, keepdims=True)
        result = inverse_ref[rows] * (grad - jnp.mean(grad, axis=-1, keepdims=True) - unit * along)
        out_ref[row] = half(result)


def exchange(values):
    return lax.all_to_all(values, group_axes, split_axis=0, concat_axis=0, tiled=True)


def local(
    pair,
    cotangent,
    residue_mask,
    chain_labels,
    gain,
    projection_weight,
    bias_weight,
    output_weight,
    position_bias_table,
    adapter_down_maps,
    adapter_up_maps,
):
    own, count, channels = pair.shape
    peers = count // own
    heads = position_bias_table.shape[0]
    rank = adapter_up_maps.shape[1]
    total = own * count
    cell_rows = own * own
    bias_rows = heads * count // lanes
    adapter_rows = 8 * rank
    adapter_chunk = adapter_rows // peers
    bias_chunk = own * bias_rows
    sent = -(-(cell_rows + bias_chunk + adapter_chunk) // 8) * 8
    f32, bf16 = jnp.float32, jnp.bfloat16
    gain_row = gain.reshape(1, channels)
    bias_weight_t = bias_weight.T
    downs = jnp.swapaxes(adapter_down_maps, 1, 2)
    params = pltpu.CompilerParams(vmem_limit_bytes=56 * 1024 * 1024)

    first_send, unit, inverse = pl.pallas_call(
        before_kernel,
        out_shape=(
            jax.ShapeDtypeStruct((peers, 2 * cell_rows + bias_chunk, channels), bf16),
            jax.ShapeDtypeStruct((total, channels), f32),
            jax.ShapeDtypeStruct((total, 1), f32),
        ),
        in_specs=[smem, smem] + [vmem] * 6,
        out_specs=(vmem, vmem, vmem),
        scratch_shapes=[
            pltpu.VMEM((total, channels), f32),
            pltpu.VMEM((total, channels), f32),
            pltpu.VMEM((bias_chunk, lanes), f32),
        ],
        compiler_params=params,
        name="before",
    )(
        residue_mask, chain_labels, chain_labels.reshape(1, count), pair, cotangent, gain_row,
        bias_weight_t, position_bias_table,
    )
    first_recv = exchange(first_send)
    second_send = pl.pallas_call(
        functools.partial(middle_kernel, own=own, heads=heads, sent=sent),
        out_shape=jax.ShapeDtypeStruct((peers * sent, channels), f32),
        in_specs=[vmem] * 5,
        out_specs=vmem,
        scratch_shapes=[
            pltpu.VMEM((total, channels), f32),
            pltpu.VMEM((total, channels), bf16),
            pltpu.VMEM((total, channels), bf16),
            pltpu.VMEM((count, heads * count), f32),
            *[pltpu.VMEM((total, channels), bf16)] * 4,
            *[pltpu.VMEM((total, channels), f32)] * 6,
            pltpu.VMEM((count * bias_rows, lanes), f32),
            pltpu.VMEM((adapter_rows, channels), f32),
        ],
        compiler_params=params,
        name="middle",
    )(first_recv, projection_weight, output_weight, downs, adapter_up_maps)
    second_recv = exchange(second_send)
    third_send = pl.pallas_call(
        functools.partial(adapter_kernel, offset=cell_rows + bias_chunk),
        out_shape=jax.ShapeDtypeStruct((peers, adapter_chunk, channels), f32),
        in_specs=[vmem],
        out_specs=vmem,
        compiler_params=params,
        name="adapters",
    )(second_recv.reshape(peers, sent, channels))
    third_recv = exchange(third_send).reshape(2, 4, rank, channels)
    pair_grad = pl.pallas_call(
        functools.partial(after_kernel, sent=sent),
        out_shape=jax.ShapeDtypeStruct((own, count, channels), bf16),
        in_specs=[vmem] * 5,
        out_specs=vmem,
        scratch_shapes=[
            pltpu.VMEM((total, channels), f32),
            pltpu.VMEM((bias_chunk, lanes), f32),
        ],
        compiler_params=params,
        name="after",
    )(second_recv, unit, inverse, gain_row, bias_weight_t)
    return (pair_grad, jnp.swapaxes(third_recv[0], 1, 2), third_recv[1])


def solution(mesh):
    return jax.shard_map(
        local,
        mesh=mesh,
        in_specs=(
            P(("groups", "dap", "sub"), None, None),
            P(("groups", "dap", "sub"), None, None),
            P("groups"),
            P("groups"),
            P(),
            P(),
            P(),
            P(),
            P(),
            P(),
            P(),
        ),
        out_specs=(
            P(("groups", "dap", "sub"), None, None),
            P("groups", None, None),
            P("groups", None, None),
        ),
        check_vma=False,
    )
```

time: 143 us -> 50.7 us (0.35)
  blocking collectives: 90.9 us -> 30.2 us
  matrix products: 24.1 us -> 0 us
  Pallas kernels: 0 us -> 10.6 us
  local copies, waits for them, and re-layouts: 9.26 us -> 0.63 us
  starting transfers between devices: 11 us -> 3.49 us
  other arithmetic: 2.39 us -> 0 us
    psum x1 -> x0, blocking collectives: 59.6 us -> none  [local(): whole_grad = lax.psum(bias_grad, ('dap', 'sub'))]
    dot_general x151 -> x0, matrix products: 24.1 us -> none  [the longest x36 5.44 us: adapted(): jnp.dot(reduced_update, adapter_up_maps[projection_index].astype(jnp.bflo...]
    all_gather x1 -> x0, blocking collectives: 21.8 us -> none  [local(): lax.all_gather(own_bias, ('dap', 'sub'), axis=1, tiled=True)]
    all_to_all x1 -> x2, blocking collectives: 9.48 us -> 30.2 us  [exchange(): lax.all_to_all(values, group_axes, split_axis=0, concat_axis=0, tiled=True)]
    pallas_call x0 -> x4, Pallas kernels: none -> 10.6 us  [the longest x1 4.7 us: local(): pl.pallas_call(functools.partial(middle_kernel, own=own, heads=heads, sen...]
    all_to_all x2 -> x1, starting transfers between devices: 11 us -> 3.49 us  [exchange(): lax.all_to_all(values, group_axes, split_axis=0, concat_axis=0, tiled=True)]
    unnamed x23 -> x0, local copies, waits for them, and re-layouts: 5.99 us -> none
    convert_element_type x17 -> x0, local copies, waits for them, and re-layouts: 1.53 us -> none  [the longest x4 0.5 us: row_attention(): adapted(2).astype(jnp.bfloat16).reshape(key_count, head_count, head_width)]
  transfers between devices with their start and end apart: 2 -> 1, of which waited for: 1 -> 1; matrix products, arithmetic and copies ran while one was open for 1% -> 0% of each run, Pallas kernels for 0% -> 4%
where the time goes in v1:
time: 50.7 us; the launch traced here: 50.3 us
  blocking collectives  30.2 us (60%)
  Pallas kernels  10.6 us (21%)
  waiting for transfers between devices  4.72 us (9%)
  starting transfers between devices  3.49 us (7%)
  between operations  0.64 us (1%)
  local copies, waits for them, and re-layouts  0.63 us (1%)
    all_to_all x2, blocking collectives, exchange(): lax.all_to_all(values, group_axes, split_axis=0, concat_axis=0, tiled=True)  30.2 us
    all_to_all x1, waiting for transfers between devices, exchange(): lax.all_to_all(values, group_axes, split_axis=0, concat_axis=0, tiled=True)  4.72 us
    pallas_call x1, Pallas kernels, local(): pl.pallas_call(functools.partial(middle_kernel, own=own, heads=heads, sen...  4.7 us
    all_to_all x1, starting transfers between devices, exchange(): lax.all_to_all(values, group_axes, split_axis=0, concat_axis=0, tiled=True)  3.49 us
    pallas_call x1, Pallas kernels, local(): pl.pallas_call(before_kernel, out_shape=(jax.ShapeDtypeStruct((peers, 2 *...  2.18 us
    pallas_call x1, Pallas kernels, local(): pl.pallas_call(functools.partial(after_kernel, sent=sent), out_shape=jax....  2.14 us
    pallas_call x1, Pallas kernels, local(): pl.pallas_call(functools.partial(adapter_kernel, offset=cell_rows + bias_...  1.6 us
  transfers between devices with their start and end apart: 1, of which 1 were waited for; matrix products, arithmetic and copies ran while one was open for 0% of the time, Pallas kernels for 4%

profile of v1, /device:TPU:0, one launch (start us, length us, event | category | flops | bytes accessed | tf_op | source)
XLA Modules:
  0.0 50.3 jit_solution(12576878907991260759)
XLA Ops:
  0.6 2.2 %before.1 = (bf16[16,40,128]{2,1,0:T(8,128)(2,1)}, f32[256,128]{1,0:T(8,128)}, f32[256,1]{1,0:T(8,128)}) custom-call(s32[64]{0:T(128)} %mask_ref.1, s32[64]{0:T(128)} %label_ref.1, s32[1,64]{1,0:T(1,128)} %bitcast.17, bf16[4,64,128]{2,1,0:T(8,128)(2,1)} %pair_ref.1, bf16[4,64,128]{2,1,0:T(8,128)(2,1)} %cot_ref.1, f32[1,128]{1,0:T(1,128)} %bitcast.18, ...), custom_call_target="tpu_custom_call" | custom-call | tf_op jit(solution)/shard_map/before/pallas_call | solution.py:344
  2.8 15.9 %all_to_all.21.recv_ref = bf16[16,40,128]{2,1,0:T(8,128)(2,1)} all-to-all(bf16[16,40,128]{2,1,0:T(8,128)(2,1)} %get-tuple-element.6), channel_id=1, replica_groups=mesh['groups'=2,'dap'=4,'sub'=4] {'dap','sub'}, dimensions={0} | all-to-all | bytes 327680 | tf_op jit(solution)/shard_map/all_to_all | solution.py:311
  18.7 4.7 %middle.1 = f32[512,128]{1,0:T(8,128)} custom-call(bf16[16,40,128]{2,1,0:T(8,128)(2,1)} %all_to_all.21.recv_ref, bf16[4,128,128]{2,1,0:T(8,128)(2,1)} %weight_ref.1, bf16[128,128]{1,0:T(8,128)(2,1)} %out_weight_ref.1, bf16[4,16,128]{2,1,0:T(8,128)(2,1)} %bitcast.14, bf16[4,16,128]{2,1,0:T(8,128)(2,1)} %up_ref.1), custom_call_target="tpu_custom_call" | custom-call | tf_op jit(solution)/shard_map/middle/pallas_call | solution.py:365
  23.4 14.2 %all_to_all.22.recv_ref = f32[16,32,128]{2,1,0:T(8,128)} all-to-all(f32[16,32,128]{2,1,0:T(8,128)} %bitcast.11), channel_id=1, replica_groups=mesh['groups'=2,'dap'=4,'sub'=4] {'dap','sub'}, dimensions={0} | all-to-all | bytes 524288 | tf_op jit(solution)/shard_map/all_to_all | solution.py:311
  37.7 1.6 %adapters.1 = f32[16,8,128]{2,1,0:T(8,128)} custom-call(f32[16,32,128]{2,1,0:T(8,128)} %all_to_all.22.recv_ref), custom_call_target="tpu_custom_call" | custom-call | tf_op jit(solution)/shard_map/adapters/pallas_call | solution.py:384
  39.3 3.5 %all-to-all-start.2 = ((f32[16,8,128]{2,1,0:T(8,128)}), f32[16,8,128]{2,1,0:T(8,128)S(1)}, u32[]{:S(2)}, u32[]{:S(2)}) async-start(f32[16,8,128]{2,1,0:T(8,128)} %adapters.1), calls=%async_computation.2 | async-start | bytes 131072 | tf_op jit(solution)/shard_map/all_to_all | solution.py:311
  42.8 2.1 %after.1 = bf16[4,64,128]{2,1,0:T(8,128)(2,1)} custom-call(f32[512,128]{1,0:T(8,128)} %bitcast.10, f32[256,128]{1,0:T(8,128)} %get-tuple-element.7.unit_ref, f32[256,1]{1,0:T(8,128)} %get-tuple-element.8.inverse_ref, f32[1,128]{1,0:T(1,128)} %bitcast.19, bf16[4,128]{1,0:T(4,128)(2,1)} %bitcast.16), custom_call_target="tpu_custom_call" | custom-call | tf_op jit(solution)/shard_map/after/pallas_call | solution.py:393
  44.9 4.7 %all-to-all-done.2 = f32[16,8,128]{2,1,0:T(8,128)S(1)} async-done(((f32[16,8,128]{2,1,0:T(8,128)}), f32[16,8,128]{2,1,0:T(8,128)S(1)}, u32[]{:S(2)}, u32[]{:S(2)}) %all-to-all-start.2) | async-done | bytes 65568 | tf_op jit(solution)/shard_map/all_to_all | solution.py:311
  49.6 0.6 %fusion = (f32[8,8,128]{2,1,0:T(8,128)}, f32[8,8,128]{2,1,0:T(8,128)}) fusion(f32[16,8,128]{2,1,0:T(8,128)S(1)} %all-to-all-done.2), kind=kLoop, calls=%fused_computation | loop fusion | bytes 131072 | tf_op jit(solution)/shard_map/slice | solution.py:405
Async XLA Ops:
  39.3 10.4 %all-to-all-start.2 = ((f32[16,8,128]{2,1,0:T(8,128)}), f32[16,8,128]{2,1,0:T(8,128)S(1)}, u32[]{:S(2)}, u32[]{:S(2)}) async-start(f32[16,8,128]{2,1,0:T(8,128)} %adapters.1), calls=%async_computation.2 | async-start | bytes 131072 | tf_op jit(solution)/shard_map/all_to_all | solution.py:311

commit v2 on v1

--- a/solution.py
+++ b/solution.py
@@ -31,6 +31,10 @@
 
 def half(values):
     return values.astype(jnp.bfloat16)
+
+
+def whole(values):
+    return half(values).astype(jnp.float32)
 
 
 def repeat(count, body):
@@ -102,10 +106,10 @@
 
 def middle_kernel(
     recv_ref, weight_ref, out_weight_ref, down_ref, up_ref,
-    send_ref,
-    rows_ref, x_ref, u_ref, bias_ref, q_ref, k_ref, v_ref, da_ref, gate_ref, dgated_ref,
-    att_ref, dq_ref, dk_ref, dv_ref, bias_grad_ref, adapter_ref,
-    *, own, heads, sent,
+    send_ref, keep_ref, give_ref,
+    rows_ref, x_ref, u_ref, bias_ref, q_ref, k_ref, v_ref, da_ref, da2_ref, gate_ref, dgated_ref,
+    att_ref, dq_ref, dk_ref, dv_ref, bias_grad_ref, adapter_ref, cells_ref,
+    *, own, heads,
 ):
     peers = recv_ref.shape[0]
     channels = recv_ref.shape[2]
@@ -140,10 +144,11 @@
             low = half(nt(x, downs[index]))
             target[rows] = half(nn(x, weights[index]) + nn(low, ups[index]))
         gate = jax.nn.sigmoid(nn(x, weights[3]))
-        dgated = half(nt(u, out_weight_ref[...]) + nn(half(nt(u, ups[3])), downs[3])).astype(jnp.float32)
+        dgated = half(whole(nt(u, out_weight_ref[...])) + whole(nn(half(nt(u, ups[3])), downs[3]))).astype(jnp.float32)
         gate_ref[rows] = gate
         dgated_ref[rows] = dgated
         da_ref[rows] = half(dgated * gate)
+        da2_ref[rows] = half(dgated * gate - half(dgated * gate).astype(jnp.float32))
 
     repeat(total // block, project)
 
@@ -166,6 +171,7 @@
 
         q_wide = spread(q_ref[queries])
         da_wide = spread(da_ref[queries])
+        da2_wide = spread(da2_ref[queries])
         k_all = k_ref[keys]
         v_all = v_ref[keys]
         bias = bias_ref[:, pl.ds(column, block)]
@@ -174,15 +180,16 @@
         powers = jnp.exp(scores - jnp.max(scores, axis=0, keepdims=True))
         chances = powers / jnp.sum(powers, axis=0, keepdims=True)
         rounded = half(chances)
-        dchances = half(nt(v_all, da_wide)).astype(jnp.float32)
+        dchances = half(nt(v_all, da_wide)+nt(v_all, da2_wide)).astype(jnp.float32)
         inner = dchances * chances
         dscores = inner - chances * jnp.sum(inner, axis=0, keepdims=True)
         dscores = jnp.where(valid, dscores, 0.0)
         scaled = half(dscores * scale)
+        rest = half(dscores * scale - scaled.astype(jnp.float32))
         return (
             queries, keys, column,
-            collect(tn(rounded, v_all)), collect(tn(scaled, k_all)),
-            nn(scaled, q_wide), nn(rounded, da_wide), dscores,
+            collect(tn(rounded, v_all)), collect(tn(scaled, k_all) + tn(rest, k_all)),
+            nn(scaled, q_wide) + nn(rest, q_wide), nn(rounded, da_wide)+nn(rounded, da2_wide), dscores,
         )
 
     if blocks == 1:
@@ -231,12 +238,12 @@
         dlow_out = half(nt(ups[3], u))
         downs_grad = [None] * 3 + [nn(dlow_out, gated)]
         ups_grad = [None] * 3 + [nn(low_out, u)]
-        grad = nt(dgate, weights[3])
+        grad = whole(nt(dgate, weights[3]))
         for index, source in enumerate((dq_ref, dk_ref, dv_ref)):
             dproj = half(source[rows])
             ups_grad[index] = nn(half(nt(downs[index], x)), dproj)
             downs_grad[index] = nn(half(nt(ups[index], dproj)), x)
-            grad = grad + nt(dproj, weights[index]) + nn(half(nt(dproj, ups[index])), downs[index])
+            grad = grad + whole(nt(dproj, weights[index])) + whole(nn(half(nt(dproj, ups[index])), downs[index]))
         for index in range(4):
             adapter_ref[index * rank : (index + 1) * rank] += downs_grad[index]
             adapter_ref[(4 + index) * rank : (5 + index) * rank] += ups_grad[index]
@@ -244,45 +251,64 @@
 
     repeat(total // block, finish)
 
+    bias_chunk = own * bias_rows
     for row in range(own):
         for place in range(own):
-            send_ref[pl.ds(row * own + place, peers, stride=sent)] = rows_ref[
+            cells_ref[pl.ds(row * own + place, peers, stride=cell_rows)] = rows_ref[
                 pl.ds(place * count + row, peers, stride=own)
             ]
-    bias_chunk = own * bias_rows
-    adapter_chunk = adapter_ref.shape[0] // peers
+    send_ref[:, 0:cell_rows] = half(cells_ref[...]).reshape(peers, cell_rows, channels)
+    send_ref[:, cell_rows:] = half(bias_grad_ref[...]).reshape(peers, bias_chunk, lanes)
+    side = lax.rem(lax.axis_index("sub"), 2) == 0
+    split = adapter_ref.shape[0] // 2
+    keep_ref[...] = jnp.where(side, adapter_ref[:split], adapter_ref[split:])
+    give_ref[...] = jnp.where(side, adapter_ref[split:], adapter_ref[:split])
+
+
+def pack_kernel(cells_ref, keep_ref, taken_ref, send_ref):
+    peers, rows, _ = cells_ref.shape
+    send_ref[:, :rows] = cells_ref[...]
+    summed = half(keep_ref[...] + taken_ref[...])
+    quarter = summed.shape[0] // 2
     for peer in range(peers):
-        base = peer * sent + cell_rows
-        send_ref[base : base + bias_chunk] = bias_grad_ref[peer * bias_chunk : (peer + 1) * bias_chunk]
-        base = base + bias_chunk
-        send_ref[base : base + adapter_chunk] = adapter_ref[peer * adapter_chunk : (peer + 1) * adapter_chunk]
-
-
-def adapter_kernel(recv_ref, send_ref, *, offset):
-    peers = recv_ref.shape[0]
-    chunk = send_ref.shape[1]
-    send_ref[...] = jnp.broadcast_to(
-        jnp.sum(recv_ref[:, offset : offset + chunk], axis=0, keepdims=True), send_ref.shape
-    )
+        side = peer % 2
+        send_ref[peer, rows:] = summed[side * quarter : (side + 1) * quarter]
+
+
+def adapter_kernel(recv_ref, out_ref, *, offset):
+    quarter = out_ref.shape[0] // 2
+    for side in range(2):
+        total = recv_ref[side, offset:].astype(jnp.float32)
+        for peer in range(side + 2, recv_ref.shape[0], 2):
+            total = total + recv_ref[peer, offset:].astype(jnp.float32)
+        out_ref[side * quarter : (side + 1) * quarter] = total
 
 
 def after_kernel(
-    recv_ref, unit_ref, inverse_ref, gain_ref, bias_weight_ref, out_ref, rows_ref, bias_ref, *, sent
+    recv_ref, mine_ref, theirs_ref, unit_ref, inverse_ref, gain_ref, bias_weight_ref,
+    out_ref, down_ref, up_ref, rows_ref, cells_ref, bias_ref,
 ):
     own, count, channels = out_ref.shape
     peers = count // own
     heads = bias_weight_ref.shape[0]
     cell_rows = own * own
     bias_rows = heads * count // lanes
+    side = lax.rem(lax.axis_index("sub"), 2) == 0
+    quarter = mine_ref.shape[0] // 2
+    for index, ref in enumerate((down_ref, up_ref)):
+        mine = mine_ref[index * quarter : (index + 1) * quarter]
+        theirs = theirs_ref[index * quarter : (index + 1) * quarter]
+        ref[:quarter] = jnp.where(side, mine, theirs)
+        ref[quarter:] = jnp.where(side, theirs, mine)
+    cells_ref[...] = recv_ref[:, :cell_rows].astype(jnp.float32).reshape(own * count, channels)
     for row in range(own):
         for place in range(own):
-            rows_ref[pl.ds(row * count + place, peers, stride=own)] = recv_ref[
-                pl.ds(row * own + place, peers, stride=sent)
+            rows_ref[pl.ds(row * count + place, peers, stride=own)] = cells_ref[
+                pl.ds(row * own + place, peers, stride=cell_rows)
             ]
-    summed = recv_ref[cell_rows : cell_rows + own * bias_rows]
+    summed = recv_ref[0, cell_rows : cell_rows + own * bias_rows].astype(jnp.float32)
     for peer in range(1, peers):
-        base = peer * sent + cell_rows
-        summed = summed + recv_ref[base : base + own * bias_rows]
+        summed = summed + recv_ref[peer, cell_rows : cell_rows + own * bias_rows].astype(jnp.float32)
     bias_ref[...] = summed
     for row in range(own):
         pieces = []
@@ -301,10 +327,15 @@
         bias_grad = half(jnp.concatenate(pieces, axis=0))
         rows = slice(row * count, (row + 1) * count)
         unit = unit_ref[rows]
-        grad = (rows_ref[rows] + tn(bias_grad, bias_weight_ref[...])) * gain_ref[...]
+        grad = (rows_ref[rows] + whole(tn(bias_grad, bias_weight_ref[...]))) * gain_ref[...]
         along = jnp.mean(grad * unit, axis=-1, keepdims=True)
         result = inverse_ref[rows] * (grad - jnp.mean(grad, axis=-1, keepdims=True) - unit * along)
         out_ref[row] = half(result)
+
+
+def swap_cores(values):
+    size = lax.axis_size("sub")
+    return lax.ppermute(values, "sub", [(place, place ^ 1) for place in range(size)])
 
 
 def exchange(values):
@@ -332,14 +363,13 @@
     cell_rows = own * own
     bias_rows = heads * count // lanes
     adapter_rows = 8 * rank
-    adapter_chunk = adapter_rows // peers
+    adapter_chunk = adapter_rows // 4
     bias_chunk = own * bias_rows
-    sent = -(-(cell_rows + bias_chunk + adapter_chunk) // 8) * 8
     f32, bf16 = jnp.float32, jnp.bfloat16
     gain_row = gain.reshape(1, channels)
     bias_weight_t = bias_weight.T
     downs = jnp.swapaxes(adapter_down_maps, 1, 2)
-    params = pltpu.CompilerParams(vmem_limit_bytes=56 * 1024 * 1024)
+    params = pltpu.CompilerParams(vmem_limit_bytes=(16 if total <= 1024 else 56) * 1024 * 1024)
 
     first_send, unit, inverse = pl.pallas_call(
         before_kernel,
@@ -362,47 +392,68 @@
         bias_weight_t, position_bias_table,
     )
     first_recv = exchange(first_send)
-    second_send = pl.pallas_call(
-        functools.partial(middle_kernel, own=own, heads=heads, sent=sent),
-        out_shape=jax.ShapeDtypeStruct((peers * sent, channels), f32),
+    cells, keep, give = pl.pallas_call(
+        functools.partial(middle_kernel, own=own, heads=heads),
+        out_shape=(
+            jax.ShapeDtypeStruct((peers, cell_rows + bias_chunk, channels), bf16),
+            jax.ShapeDtypeStruct((adapter_rows // 2, channels), f32),
+            jax.ShapeDtypeStruct((adapter_rows // 2, channels), f32),
+        ),
         in_specs=[vmem] * 5,
-        out_specs=vmem,
+        out_specs=(vmem,) * 3,
         scratch_shapes=[
             pltpu.VMEM((total, channels), f32),
             pltpu.VMEM((total, channels), bf16),
             pltpu.VMEM((total, channels), bf16),
             pltpu.VMEM((count, heads * count), f32),
-            *[pltpu.VMEM((total, channels), bf16)] * 4,
+            *[pltpu.VMEM((total, channels), bf16)] * 5,
             *[pltpu.VMEM((total, channels), f32)] * 6,
             pltpu.VMEM((count * bias_rows, lanes), f32),
             pltpu.VMEM((adapter_rows, channels), f32),
+            pltpu.VMEM((total, channels), f32),
         ],
         compiler_params=params,
         name="middle",
     )(first_recv, projection_weight, output_weight, downs, adapter_up_maps)
+    second_send = pl.pallas_call(
+        pack_kernel,
+        out_shape=jax.ShapeDtypeStruct((peers, cell_rows + bias_chunk + adapter_chunk, channels), bf16),
+        in_specs=[vmem] * 3,
+        out_specs=vmem,
+        compiler_params=params,
+        name="pack",
+    )(cells, keep, swap_cores(give))
     second_recv = exchange(second_send)
-    third_send = pl.pallas_call(
+    mine = pl.pallas_call(
         functools.partial(adapter_kernel, offset=cell_rows + bias_chunk),
-        out_shape=jax.ShapeDtypeStruct((peers, adapter_chunk, channels), f32),
+        out_shape=jax.ShapeDtypeStruct((adapter_rows // 2, channels), f32),
         in_specs=[vmem],
         out_specs=vmem,
         compiler_params=params,
         name="adapters",
-    )(second_recv.reshape(peers, sent, channels))
-    third_recv = exchange(third_send).reshape(2, 4, rank, channels)
-    pair_grad = pl.pallas_call(
-        functools.partial(after_kernel, sent=sent),
-        out_shape=jax.ShapeDtypeStruct((own, count, channels), bf16),
-        in_specs=[vmem] * 5,
-        out_specs=vmem,
+    )(second_recv)
+    pair_grad, down_grad, up_grad = pl.pallas_call(
+        after_kernel,
+        out_shape=(
+            jax.ShapeDtypeStruct((own, count, channels), bf16),
+            jax.ShapeDtypeStruct((adapter_rows // 2, channels), f32),
+            jax.ShapeDtypeStruct((adapter_rows // 2, channels), f32),
+        ),
+        in_specs=[vmem] * 7,
+        out_specs=(vmem,) * 3,
         scratch_shapes=[
+            pltpu.VMEM((total, channels), f32),
             pltpu.VMEM((total, channels), f32),
             pltpu.VMEM((bias_chunk, lanes), f32),
         ],
         compiler_params=params,
         name="after",
-    )(second_recv, unit, inverse, gain_row, bias_weight_t)
-    return (pair_grad, jnp.swapaxes(third_recv[0], 1, 2), third_recv[1])
+    )(second_recv, mine, swap_cores(mine), unit, inverse, gain_row, bias_weight_t)
+    return (
+        pair_grad,
+        jnp.swapaxes(down_grad.reshape(4, rank, channels), 1, 2),
+        up_grad.reshape(4, rank, channels),
+    )
 
 
 def solution(mesh):

time: 50.7 us -> 39 us (0.77)
  Pallas kernels: 10.6 us -> 5.18 us
  starting transfers between devices: 3.49 us -> 0.14 us
  waiting for transfers between devices: 4.72 us -> 2.39 us
  blocking collectives: 30.2 us -> 27.9 us
  local copies, waits for them, and re-layouts: 0.63 us -> 2.39 us
    all_to_all x1 -> x0, waiting for transfers between devices: 4.72 us -> none  [exchange(): lax.all_to_all(values, group_axes, split_axis=0, concat_axis=0, tiled=True)]
    all_to_all x1 -> x0, starting transfers between devices: 3.49 us -> none  [exchange(): lax.all_to_all(values, group_axes, split_axis=0, concat_axis=0, tiled=True)]
    pallas_call x2 -> x3, Pallas kernels: 6.84 us -> 4.01 us  [the longest x1 2.91 us: local(): pl.pallas_call(functools.partial(middle_kernel, own=own, heads=heads), ou...]
    unnamed x0 -> x22, local copies, waits for them, and re-layouts: none -> 2.39 us
    ppermute x0 -> x2, waiting for transfers between devices: none -> 2.39 us  [swap_cores(): lax.ppermute(values, 'sub', [(place, place ^ 1) for place in range(size)])]
    all_to_all x2, blocking collectives: 30.2 us -> 27.9 us  [exchange(): lax.all_to_all(values, group_axes, split_axis=0, concat_axis=0, tiled=True)]
    pallas_call x1, Pallas kernels: 1.6 us -> 0.02 us  [local(): pl.pallas_call(functools.partial(adapter_kernel, offset=cell_rows + bias_...]
    pallas_call x1, Pallas kernels: 2.18 us -> 1.14 us  [local(): pl.pallas_call(before_kernel, out_shape=(jax.ShapeDtypeStruct((peers, 2 *...]
  transfers between devices with their start and end apart: 1 -> 2, of which waited for: 1 -> 2; matrix products, arithmetic and copies ran while one was open for 0% -> 0% of each run, Pallas kernels for 4% -> 0%
where the time goes in v2:
time: 39 us; the launch traced here: 38.7 us
  blocking collectives  27.9 us (72%)
  Pallas kernels  5.18 us (13%)
  local copies, waits for them, and re-layouts  2.39 us (6%)
  waiting for transfers between devices  2.39 us (6%)
  between operations  0.75 us (2%)
    all_to_all x2, blocking collectives, exchange(): lax.all_to_all(values, group_axes, split_axis=0, concat_axis=0, tiled=True)  27.9 us
    pallas_call x1, Pallas kernels, local(): pl.pallas_call(functools.partial(middle_kernel, own=own, heads=heads), ou...  2.91 us
    unnamed x22, local copies, waits for them, and re-layouts  2.39 us
    ppermute x2, waiting for transfers between devices, swap_cores(): lax.ppermute(values, 'sub', [(place, place ^ 1) for place in range(size)])  2.39 us
    pallas_call x1, Pallas kernels, local(): pl.pallas_call(before_kernel, out_shape=(jax.ShapeDtypeStruct((peers, 2 *...  1.14 us
    pallas_call x1, Pallas kernels, local(): pl.pallas_call(after_kernel, out_shape=(jax.ShapeDtypeStruct((own, count,...  1.08 us
  transfers between devices with their start and end apart: 2, of which 2 were waited for; matrix products, arithmetic and copies ran while one was open for 0% of the time, Pallas kernels for 0%

profile of v2, /device:TPU:0, one launch (start us, length us, event | category | flops | bytes accessed | tf_op | source)
XLA Modules:
  0.0 38.7 jit_solution(15468335069398677494)
XLA Ops:
  0.6 0.0 copy-start.9
  0.6 0.0 copy-start.10
  0.7 0.0 copy-start.7
  0.7 0.0 copy-start.6
  0.7 0.0 copy-start.8
  0.7 0.6 %copy-done.9 = f32[128]{0:T(128)S(1)} copy-done((f32[128]{0:T(128)S(1)}, f32[128]{0:T(128)}, u32[]{:S(2)}) %copy-start.9) | copy-done | bytes 536
  1.3 0.0 copy-done.10
  1.3 0.0 copy-done.7
  1.3 0.0 copy-done.6
  1.4 0.0 copy-done.8
  1.4 0.0 copy-start.1
  1.4 0.8 %copy-done.1 = bf16[4,64,128]{2,1,0:T(8,128)(2,1)S(1)} copy-done((bf16[4,64,128]{2,1,0:T(8,128)(2,1)S(1)}, bf16[4,64,128]{2,1,0:T(8,128)(2,1)}, u32[]{:S(2)}) %copy-start.1) | copy-done | bytes 65560
  2.2 0.0 copy-start.2
  2.2 0.8 %copy-done.2 = bf16[4,64,128]{2,1,0:T(8,128)(2,1)S(1)} copy-done((bf16[4,64,128]{2,1,0:T(8,128)(2,1)S(1)}, bf16[4,64,128]{2,1,0:T(8,128)(2,1)}, u32[]{:S(2)}) %copy-start.2) | copy-done | bytes 65560
  3.0 1.1 %before.1 = (bf16[16,40,128]{2,1,0:T(8,128)(2,1)S(1)}, f32[256,128]{1,0:T(8,128)S(1)}, f32[256,1]{1,0:T(8,128)S(1)}) custom-call(s32[64]{0:T(128)S(1)} %copy-done.10, s32[64]{0:T(128)S(1)} %copy-done.8, s32[1,64]{1,0:T(1,128)S(1)} %bitcast.11, bf16[4,64,128]{2,1,0:T(8,128)(2,1)S(1)} %copy-done.1, bf16[4,64,128]{2,1,0:T(8,128)(2,1)S(1)} %copy-done.2, ...), custom_call_target="tpu_custom_call" | custom-call | tf_op jit(solution)/shard_map/before/pallas_call | solution.py:374
  4.2 0.0 copy-start
  4.2 0.0 copy-start.3
  4.2 0.0 copy-start.4
  4.2 0.0 copy-start.5
  4.2 15.8 %all_to_all.10.recv_ref = bf16[16,40,128]{2,1,0:T(8,128)(2,1)S(1)} all-to-all(bf16[16,40,128]{2,1,0:T(8,128)(2,1)S(1)} %get-tuple-element.12), channel_id=1, replica_groups=mesh['groups'=2,'dap'=4,'sub'=4] {'dap','sub'}, dimensions={0} | all-to-all | bytes 327680 | tf_op jit(solution)/shard_map/all_to_all | solution.py:342
  20.0 0.0 copy-done
  20.0 0.0 copy-done.3
  20.0 0.0 copy-done.4
  20.0 0.0 copy-done.5
  20.0 2.9 %middle.1 = (bf16[16,24,128]{2,1,0:T(8,128)(2,1)S(1)}, f32[64,128]{1,0:T(8,128)S(1)}, f32[64,128]{1,0:T(8,128)S(1)}) custom-call(bf16[16,40,128]{2,1,0:T(8,128)(2,1)S(1)} %all_to_all.10.recv_ref, bf16[4,128,128]{2,1,0:T(8,128)(2,1)S(1)} %copy-done, bf16[128,128]{1,0:T(8,128)(2,1)S(1)} %copy-done.3, bf16[4,16,128]{2,1,0:T(8,128)(2,1)S(1)} %bitcast.8, ...), custom_call_target="tpu_custom_call" | custom-call | tf_op jit(solution)/shard_map/middle/pallas_call | solution.py:395
  22.9 0.1 collective-permute-start
  23.0 1.2 %collective-permute-done.taken_ref = f32[64,128]{1,0:T(8,128)S(1)} collective-permute-done((f32[64,128]{1,0:T(8,128)S(1)}, f32[64,128]{1,0:T(8,128)S(1)}, u32[]{:S(2)}, u32[]{:S(2)}) %collective-permute-start) | collective-permute-done | bytes 32800 | tf_op jit(solution)/shard_map/ppermute | solution.py:338
  24.2 12.1 %all_to_all.11.recv_ref = bf16[16,56,128]{2,1,0:T(8,128)(2,1)S(1)} all-to-all(bf16[16,56,128]{2,1,0:T(8,128)(2,1)S(1)} %pack.1), channel_id=1, replica_groups=mesh['groups'=2,'dap'=4,'sub'=4] {'dap','sub'}, dimensions={0} | all-to-all | bytes 458752 | tf_op jit(solution)/shard_map/all_to_all | solution.py:342
  36.4 0.1 collective-permute-start.1
  36.4 1.2 %collective-permute-done.1.theirs_ref = f32[64,128]{1,0:T(8,128)S(1)} collective-permute-done((f32[64,128]{1,0:T(8,128)S(1)}, f32[64,128]{1,0:T(8,128)S(1)}, u32[]{:S(2)}, u32[]{:S(2)}) %collective-permute-start.1) | collective-permute-done | bytes 32800 | tf_op jit(solution)/shard_map/ppermute | solution.py:338
  37.6 1.1 %after.1 = (bf16[4,64,128]{2,1,0:T(8,128)(2,1)}, f32[64,128]{1,0:T(8,128)}, f32[64,128]{1,0:T(8,128)}) custom-call(bf16[16,56,128]{2,1,0:T(8,128)(2,1)S(1)} %all_to_all.11.recv_ref, f32[64,128]{1,0:T(8,128)S(1)} %adapters.1.mine_ref, f32[64,128]{1,0:T(8,128)S(1)} %collective-permute-done.1.theirs_ref, f32[256,128]{1,0:T(8,128)S(1)} %get-tuple-element.16.unit_ref, ...), custom_call_target="tpu_custom_call" | custom-call | tf_op jit(solution)/shard_map/after/pallas_call | solution.py:435
  (2 shorter events, 0.0 us)
Async XLA Ops:
  0.6 0.7 %copy-start.9 = (f32[128]{0:T(128)S(1)}, f32[128]{0:T(128)}, u32[]{:S(2)}) copy-start(f32[128]{0:T(128)} %param.15) | copy-start | bytes 1540
  0.6 0.7 %copy-start.10 = (s32[64]{0:T(128)S(1)}, s32[64]{0:T(128)}, u32[]{:S(2)}) copy-start(s32[64]{0:T(128)} %mask_ref.1) | copy-start | bytes 772
  0.7 0.7 %copy-start.7 = (f32[4,66]{1,0:T(4,128)S(1)}, f32[4,66]{1,0:T(4,128)}, u32[]{:S(2)}) copy-start(f32[4,66]{1,0:T(4,128)} %table_ref.1) | copy-start | bytes 3172
  0.7 0.7 %copy-start.6 = (bf16[128,4]{0,1:T(4,128)(2,1)S(1)}, bf16[128,4]{0,1:T(4,128)(2,1)}, u32[]{:S(2)}) copy-start(bf16[128,4]{0,1:T(4,128)(2,1)} %param.17) | copy-start | bytes 3076
  0.7 0.7 %copy-start.8 = (s32[64]{0:T(128)S(1)}, s32[64]{0:T(128)}, u32[]{:S(2)}) copy-start(s32[64]{0:T(128)} %label_ref.1) | copy-start | bytes 772
  1.4 0.8 %copy-start.1 = (bf16[4,64,128]{2,1,0:T(8,128)(2,1)S(1)}, bf16[4,64,128]{2,1,0:T(8,128)(2,1)}, u32[]{:S(2)}) copy-start(bf16[4,64,128]{2,1,0:T(8,128)(2,1)} %pair_ref.1) | copy-start | bytes 196612
  2.2 0.8 %copy-start.2 = (bf16[4,64,128]{2,1,0:T(8,128)(2,1)S(1)}, bf16[4,64,128]{2,1,0:T(8,128)(2,1)}, u32[]{:S(2)}) copy-start(bf16[4,64,128]{2,1,0:T(8,128)(2,1)} %cot_ref.1) | copy-start | bytes 196612
  4.2 15.8 %copy-start = (bf16[4,128,128]{2,1,0:T(8,128)(2,1)S(1)}, bf16[4,128,128]{2,1,0:T(8,128)(2,1)}, u32[]{:S(2)}) copy-start(bf16[4,128,128]{2,1,0:T(8,128)(2,1)} %weight_ref.1) | copy-start | bytes 393220
  4.2 15.8 %copy-start.3 = (bf16[128,128]{1,0:T(8,128)(2,1)S(1)}, bf16[128,128]{1,0:T(8,128)(2,1)}, u32[]{:S(2)}) copy-start(bf16[128,128]{1,0:T(8,128)(2,1)} %out_weight_ref.1) | copy-start | bytes 98308
  4.2 15.8 %copy-start.4 = (bf16[4,128,16]{1,2,0:T(8,128)(2,1)S(1)}, bf16[4,128,16]{1,2,0:T(8,128)(2,1)}, u32[]{:S(2)}) copy-start(bf16[4,128,16]{1,2,0:T(8,128)(2,1)} %param.20) | copy-start | bytes 49156
  4.2 15.8 %copy-start.5 = (bf16[4,16,128]{2,1,0:T(8,128)(2,1)S(1)}, bf16[4,16,128]{2,1,0:T(8,128)(2,1)}, u32[]{:S(2)}) copy-start(bf16[4,16,128]{2,1,0:T(8,128)(2,1)} %up_ref.1) | copy-start | bytes 49156
  22.9 1.3 %collective-permute-start = (f32[64,128]{1,0:T(8,128)S(1)}, f32[64,128]{1,0:T(8,128)S(1)}, u32[]{:S(2)}, u32[]{:S(2)}) collective-permute-start(f32[64,128]{1,0:T(8,128)S(1)} %get-tuple-element.15), channel_id=1, source_target_pairs={{0,1},{1,0},{2,3},{3,2},{4,5},{5,4},{6,7},{7,6},{8,9},{9,8},{10,11... | collective-permute-start | bytes 98312 | tf_op jit(solution)/shard_map/ppermute | solution.py:338
  36.4 1.3 %collective-permute-start.1 = (f32[64,128]{1,0:T(8,128)S(1)}, f32[64,128]{1,0:T(8,128)S(1)}, u32[]{:S(2)}, u32[]{:S(2)}) collective-permute-start(f32[64,128]{1,0:T(8,128)S(1)} %adapters.1.mine_ref), channel_id=1, source_target_pairs={{0,1},{1,0},{2,3},{3,2},{4,5},{5,4},{6,7},{7,6},{8,9},{9,8},{10,11... | collective-permute-start | bytes 98312 | tf_op jit(solution)/shard_map/ppermute | solution.py:338

commit v3 on v2

--- a/solution.py
+++ b/solution.py
@@ -14,7 +14,7 @@
 masked_bias = -3e38
 group_axes = ("dap", "sub")
 vmem = pl.BlockSpec(memory_space=pltpu.VMEM)
-smem = pl.BlockSpec(memory_space=pltpu.SMEM)
+hbm = pl.BlockSpec(memory_space=pltpu.HBM)
 
 
 def nn(left, right):
@@ -31,10 +31,6 @@
 
 def half(values):
     return values.astype(jnp.bfloat16)
-
-
-def whole(values):
-    return half(values).astype(jnp.float32)
 
 
 def repeat(count, body):
@@ -45,9 +41,21 @@
 
 
 def before_kernel(
-    mask_ref, label_ref, label_row_ref, pair_ref, cot_ref, gain_ref, bias_weight_ref, table_ref,
-    send_ref, unit_ref, inverse_ref, normed_ref, cells_ref, bias_ref,
+    mask_hbm, label_hbm, label_row_hbm, pair_hbm, cot_hbm, gain_hbm, bias_weight_hbm, table_hbm,
+    send_ref, unit_ref, inverse_ref, gain_ref, bias_weight_ref,
+    normed_ref, cells_ref, bias_ref, mask_ref, label_ref, label_row_ref, pair_ref, cot_ref, table_ref, sems,
 ):
+    copies = [
+        pltpu.make_async_copy(source, target, sems.at[index])
+        for index, (source, target) in enumerate((
+            (pair_hbm, pair_ref), (mask_hbm, mask_ref), (label_hbm, label_ref), (label_row_hbm, label_row_ref),
+            (gain_hbm, gain_ref), (bias_weight_hbm, bias_weight_ref), (table_hbm, table_ref), (cot_hbm, cot_ref),
+        ))
+    ]
+    for copy in copies:
+        copy.start()
+    for copy in copies[:-1]:
+        copy.wait()
     own, count, channels = pair_ref.shape
     peers = count // own
     heads, bins = table_ref.shape
@@ -97,6 +105,7 @@
         return half(cells_ref[...]).reshape(peers, cell_rows, channels)
 
     send_ref[:, 0:cell_rows] = scatter()
+    copies[-1].wait()
     for row in range(own):
         normed_ref[row * count : (row + 1) * count] = cot_ref[row].astype(jnp.float32)
     send_ref[:, cell_rows : 2 * cell_rows] = scatter()
@@ -144,11 +153,13 @@
             low = half(nt(x, downs[index]))
             target[rows] = half(nn(x, weights[index]) + nn(low, ups[index]))
         gate = jax.nn.sigmoid(nn(x, weights[3]))
-        dgated = half(whole(nt(u, out_weight_ref[...])) + whole(nn(half(nt(u, ups[3])), downs[3]))).astype(jnp.float32)
+        dgated = nt(u, out_weight_ref[...]) + nn(half(nt(u, ups[3])), downs[3])
         gate_ref[rows] = gate
         dgated_ref[rows] = dgated
-        da_ref[rows] = half(dgated * gate)
-        da2_ref[rows] = half(dgated * gate - half(dgated * gate).astype(jnp.float32))
+        dattended = dgated * gate
+        leading = half(dattended)
+        da_ref[rows] = leading
+        da2_ref[rows] = half(dattended - leading.astype(jnp.float32))
 
     repeat(total // block, project)
 
@@ -180,7 +191,7 @@
         powers = jnp.exp(scores - jnp.max(scores, axis=0, keepdims=True))
         chances = powers / jnp.sum(powers, axis=0, keepdims=True)
         rounded = half(chances)
-        dchances = half(nt(v_all, da_wide)+nt(v_all, da2_wide)).astype(jnp.float32)
+        dchances = half(nt(v_all, da_wide) + nt(v_all, da2_wide)).astype(jnp.float32)
         inner = dchances * chances
         dscores = inner - chances * jnp.sum(inner, axis=0, keepdims=True)
         dscores = jnp.where(valid, dscores, 0.0)
@@ -189,7 +200,7 @@
         return (
             queries, keys, column,
             collect(tn(rounded, v_all)), collect(tn(scaled, k_all) + tn(rest, k_all)),
-            nn(scaled, q_wide) + nn(rest, q_wide), nn(rounded, da_wide)+nn(rounded, da2_wide), dscores,
+            nn(scaled, q_wide) + nn(rest, q_wide), nn(rounded, da_wide) + nn(rounded, da2_wide), dscores,
         )
 
     if blocks == 1:
@@ -238,12 +249,12 @@
         dlow_out = half(nt(ups[3], u))
         downs_grad = [None] * 3 + [nn(dlow_out, gated)]
         ups_grad = [None] * 3 + [nn(low_out, u)]
-        grad = whole(nt(dgate, weights[3]))
+        grad = nt(dgate, weights[3])
         for index, source in enumerate((dq_ref, dk_ref, dv_ref)):
             dproj = half(source[rows])
             ups_grad[index] = nn(half(nt(downs[index], x)), dproj)
             downs_grad[index] = nn(half(nt(ups[index], dproj)), x)
-            grad = grad + whole(nt(dproj, weights[index])) + whole(nn(half(nt(dproj, ups[index])), downs[index]))
+            grad = grad + nt(dproj, weights[index]) + nn(half(nt(dproj, ups[index])), downs[index])
         for index in range(4):
             adapter_ref[index * rank : (index + 1) * rank] += downs_grad[index]
             adapter_ref[(4 + index) * rank : (5 + index) * rank] += ups_grad[index]
@@ -327,7 +338,7 @@
         bias_grad = half(jnp.concatenate(pieces, axis=0))
         rows = slice(row * count, (row + 1) * count)
         unit = unit_ref[rows]
-        grad = (rows_ref[rows] + whole(tn(bias_grad, bias_weight_ref[...]))) * gain_ref[...]
+        grad = (rows_ref[rows] + tn(bias_grad, bias_weight_ref[...])) * gain_ref[...]
         along = jnp.mean(grad * unit, axis=-1, keepdims=True)
         result = inverse_ref[rows] * (grad - jnp.mean(grad, axis=-1, keepdims=True) - unit * along)
         out_ref[row] = half(result)
@@ -371,25 +382,39 @@
     downs = jnp.swapaxes(adapter_down_maps, 1, 2)
     params = pltpu.CompilerParams(vmem_limit_bytes=(16 if total <= 1024 else 56) * 1024 * 1024)
 
-    first_send, unit, inverse = pl.pallas_call(
+    first_send, unit, inverse, gain_kept, bias_weight_kept = pl.pallas_call(
         before_kernel,
         out_shape=(
             jax.ShapeDtypeStruct((peers, 2 * cell_rows + bias_chunk, channels), bf16),
             jax.ShapeDtypeStruct((total, channels), f32),
             jax.ShapeDtypeStruct((total, 1), f32),
+            jax.ShapeDtypeStruct((1, channels), f32),
+            jax.ShapeDtypeStruct((heads, channels), bf16),
         ),
-        in_specs=[smem, smem] + [vmem] * 6,
-        out_specs=(vmem, vmem, vmem),
+        in_specs=[hbm] * 8,
+        out_specs=(vmem,) * 5,
         scratch_shapes=[
             pltpu.VMEM((total, channels), f32),
             pltpu.VMEM((total, channels), f32),
             pltpu.VMEM((bias_chunk, lanes), f32),
+            pltpu.SMEM((count,), jnp.int32),
+            pltpu.SMEM((count,), jnp.int32),
+            pltpu.VMEM((1, count), jnp.int32),
+            pltpu.VMEM(pair.shape, bf16),
+            pltpu.VMEM(pair.shape, bf16),
+            pltpu.VMEM(position_bias_table.shape, f32),
+            pltpu.SemaphoreType.DMA((8,)),
         ],
         compiler_params=params,
         name="before",
     )(
-        residue_mask, chain_labels, chain_labels.reshape(1, count), pair, cotangent, gain_row,
-        bias_weight_t, position_bias_table,
+        *(
+            pltpu.with_memory_space_constraint(value, pltpu.HBM)
+            for value in (
+                residue_mask, chain_labels, chain_labels.reshape(1, count), pair, cotangent, gain_row,
+                bias_weight_t, position_bias_table,
+            )
+        )
     )
     first_recv = exchange(first_send)
     cells, keep, give = pl.pallas_call(
@@ -448,7 +473,7 @@
         ],
         compiler_params=params,
         name="after",
-    )(second_recv, mine, swap_cores(mine), unit, inverse, gain_row, bias_weight_t)
+    )(second_recv, mine, swap_cores(mine), unit, inverse, gain_kept, bias_weight_kept)
     return (
         pair_grad,
         jnp.swapaxes(down_grad.reshape(4, rank, channels), 1, 2),

time: 39 us -> 37.3 us (0.956)
  local copies, waits for them, and re-layouts: 2.39 us -> 0.03 us
  Pallas kernels: 5.18 us -> 5.96 us
    unnamed x22 -> x8, local copies, waits for them, and re-layouts: 2.39 us -> 0.03 us
    pallas_call x1, Pallas kernels: 1.14 us -> 1.57 us  [local(): pl.pallas_call(before_kernel, out_shape=(jax.ShapeDtypeStruct((peers, 2 *...]
where the time goes in v3:
time: 37.3 us; the launch traced here: 37.1 us
  blocking collectives  27.9 us (75%)
  Pallas kernels  5.96 us (16%)
  waiting for transfers between devices  2.39 us (6%)
  between operations  0.72 us (2%)
    all_to_all x2, blocking collectives, exchange(): lax.all_to_all(values, group_axes, split_axis=0, concat_axis=0, tiled=True)  27.9 us
    pallas_call x1, Pallas kernels, local(): pl.pallas_call(functools.partial(middle_kernel, own=own, heads=heads), ou...  3.26 us
    ppermute x2, waiting for transfers between devices, swap_cores(): lax.ppermute(values, 'sub', [(place, place ^ 1) for place in range(size)])  2.39 us
    pallas_call x1, Pallas kernels, local(): pl.pallas_call(before_kernel, out_shape=(jax.ShapeDtypeStruct((peers, 2 *...  1.57 us
    pallas_call x1, Pallas kernels, local(): pl.pallas_call(after_kernel, out_shape=(jax.ShapeDtypeStruct((own, count,...  1.08 us
  transfers between devices with their start and end apart: 2, of which 2 were waited for; matrix products, arithmetic and copies ran while one was open for 0% of the time, Pallas kernels for 0%

profile of v3, /device:TPU:0, one launch (start us, length us, event | category | flops | bytes accessed | tf_op | source)
XLA Modules:
  0.0 37.1 jit_solution(14033308361760255689)
XLA Ops:
  0.6 1.6 %before.1 = (bf16[16,40,128]{2,1,0:T(8,128)(2,1)S(1)}, f32[256,128]{1,0:T(8,128)S(1)}, f32[256,1]{1,0:T(8,128)S(1)}, f32[1,128]{1,0:T(1,128)S(1)}, bf16[4,128]{1,0:T(4,128)(2,1)S(1)}) custom-call(s32[64]{0:T(128)} %mask_hbm.1, s32[64]{0:T(128)} %label_hbm.1, s32[1,64]{1,0:T(1,128)} %bitcast.9, bf16[4,64,128]{2,1,0:T(8,128)(2,1)} %pair_hbm.1, ...), custom_call_target="tpu_custom_call" | custom-call | tf_op jit(solution)/shard_map/before/pallas_call | solution.py:385
  2.2 0.0 copy-start
  2.2 0.0 copy-start.1
  2.2 0.0 copy-start.2
  2.2 0.0 copy-start.3
  2.3 15.8 %all_to_all.10.recv_ref = bf16[16,40,128]{2,1,0:T(8,128)(2,1)S(1)} all-to-all(bf16[16,40,128]{2,1,0:T(8,128)(2,1)S(1)} %get-tuple-element.14), channel_id=1, replica_groups=mesh['groups'=2,'dap'=4,'sub'=4] {'dap','sub'}, dimensions={0} | all-to-all | bytes 327680 | tf_op jit(solution)/shard_map/all_to_all | solution.py:353
  18.0 0.0 copy-done
  18.0 0.0 copy-done.1
  18.0 0.0 copy-done.2
  18.0 0.0 copy-done.3
  18.0 3.3 %middle.1 = (bf16[16,24,128]{2,1,0:T(8,128)(2,1)S(1)}, f32[64,128]{1,0:T(8,128)S(1)}, f32[64,128]{1,0:T(8,128)S(1)}) custom-call(bf16[16,40,128]{2,1,0:T(8,128)(2,1)S(1)} %all_to_all.10.recv_ref, bf16[4,128,128]{2,1,0:T(8,128)(2,1)S(1)} %copy-done, bf16[128,128]{1,0:T(8,128)(2,1)S(1)} %copy-done.1, bf16[4,16,128]{2,1,0:T(8,128)(2,1)S(1)} %bitcast.8, ...), custom_call_target="tpu_custom_call" | custom-call | tf_op jit(solution)/shard_map/middle/pallas_call | solution.py:420
  21.3 0.1 collective-permute-start
  21.4 1.2 %collective-permute-done.taken_ref = f32[64,128]{1,0:T(8,128)S(1)} collective-permute-done((f32[64,128]{1,0:T(8,128)S(1)}, f32[64,128]{1,0:T(8,128)S(1)}, u32[]{:S(2)}, u32[]{:S(2)}) %collective-permute-start) | collective-permute-done | bytes 32800 | tf_op jit(solution)/shard_map/ppermute | solution.py:349
  22.6 12.1 %all_to_all.11.recv_ref = bf16[16,56,128]{2,1,0:T(8,128)(2,1)S(1)} all-to-all(bf16[16,56,128]{2,1,0:T(8,128)(2,1)S(1)} %pack.1), channel_id=1, replica_groups=mesh['groups'=2,'dap'=4,'sub'=4] {'dap','sub'}, dimensions={0} | all-to-all | bytes 458752 | tf_op jit(solution)/shard_map/all_to_all | solution.py:353
  34.7 0.1 collective-permute-start.1
  34.8 1.2 %collective-permute-done.1.theirs_ref = f32[64,128]{1,0:T(8,128)S(1)} collective-permute-done((f32[64,128]{1,0:T(8,128)S(1)}, f32[64,128]{1,0:T(8,128)S(1)}, u32[]{:S(2)}, u32[]{:S(2)}) %collective-permute-start.1) | collective-permute-done | bytes 32800 | tf_op jit(solution)/shard_map/ppermute | solution.py:349
  36.0 1.1 %after.1 = (bf16[4,64,128]{2,1,0:T(8,128)(2,1)}, f32[64,128]{1,0:T(8,128)}, f32[64,128]{1,0:T(8,128)}) custom-call(bf16[16,56,128]{2,1,0:T(8,128)(2,1)S(1)} %all_to_all.11.recv_ref, f32[64,128]{1,0:T(8,128)S(1)} %adapters.1.mine_ref, f32[64,128]{1,0:T(8,128)S(1)} %collective-permute-done.1.theirs_ref, f32[256,128]{1,0:T(8,128)S(1)} %get-tuple-element.18.unit_ref, ...), custom_call_target="tpu_custom_call" | custom-call | tf_op jit(solution)/shard_map/after/pallas_call | solution.py:460
  (2 shorter events, 0.0 us)
Async XLA Ops:
  2.2 15.8 %copy-start = (bf16[4,128,128]{2,1,0:T(8,128)(2,1)S(1)}, bf16[4,128,128]{2,1,0:T(8,128)(2,1)}, u32[]{:S(2)}) copy-start(bf16[4,128,128]{2,1,0:T(8,128)(2,1)} %weight_ref.1) | copy-start | bytes 393220
  2.2 15.8 %copy-start.1 = (bf16[128,128]{1,0:T(8,128)(2,1)S(1)}, bf16[128,128]{1,0:T(8,128)(2,1)}, u32[]{:S(2)}) copy-start(bf16[128,128]{1,0:T(8,128)(2,1)} %out_weight_ref.1) | copy-start | bytes 98308
  2.2 15.8 %copy-start.2 = (bf16[4,128,16]{1,2,0:T(8,128)(2,1)S(1)}, bf16[4,128,16]{1,2,0:T(8,128)(2,1)}, u32[]{:S(2)}) copy-start(bf16[4,128,16]{1,2,0:T(8,128)(2,1)} %param.20) | copy-start | bytes 49156
  2.2 15.8 %copy-start.3 = (bf16[4,16,128]{2,1,0:T(8,128)(2,1)S(1)}, bf16[4,16,128]{2,1,0:T(8,128)(2,1)}, u32[]{:S(2)}) copy-start(bf16[4,16,128]{2,1,0:T(8,128)(2,1)} %up_ref.1) | copy-start | bytes 49156
  21.3 1.3 %collective-permute-start = (f32[64,128]{1,0:T(8,128)S(1)}, f32[64,128]{1,0:T(8,128)S(1)}, u32[]{:S(2)}, u32[]{:S(2)}) collective-permute-start(f32[64,128]{1,0:T(8,128)S(1)} %get-tuple-element.17), channel_id=1, source_target_pairs={{0,1},{1,0},{2,3},{3,2},{4,5},{5,4},{6,7},{7,6},{8,9},{9,8},{10,11... | collective-permute-start | bytes 98312 | tf_op jit(solution)/shard_map/ppermute | solution.py:349
  34.7 1.3 %collective-permute-start.1 = (f32[64,128]{1,0:T(8,128)S(1)}, f32[64,128]{1,0:T(8,128)S(1)}, u32[]{:S(2)}, u32[]{:S(2)}) collective-permute-start(f32[64,128]{1,0:T(8,128)S(1)} %adapters.1.mine_ref), channel_id=1, source_target_pairs={{0,1},{1,0},{2,3},{3,2},{4,5},{5,4},{6,7},{7,6},{8,9},{9,8},{10,11... | collective-permute-start | bytes 98312 | tf_op jit(solution)/shard_map/ppermute | solution.py:349

commit v4 on v3

--- a/solution.py
+++ b/solution.py
@@ -113,11 +113,30 @@
     send_ref[:, 2 * cell_rows :] = jnp.broadcast_to(bias_all[None], (peers, *bias_all.shape))
 
 
+def stacked(maps_ref, count):
+    return jnp.concatenate([maps_ref[index] for index in range(count)], axis=0)
+
+
+def blocked(maps_ref, count):
+    empty = jnp.zeros_like(maps_ref[0])
+    return jnp.concatenate(
+        [
+            jnp.concatenate([maps_ref[index] if place == index else empty for place in range(count)], axis=1)
+            for index in range(count)
+        ],
+        axis=0,
+    )
+
+
+def beside(weight_ref, first):
+    return jnp.concatenate([weight_ref[first], weight_ref[first + 1]], axis=1)
+
+
 def middle_kernel(
     recv_ref, weight_ref, out_weight_ref, down_ref, up_ref,
-    send_ref, keep_ref, give_ref,
-    rows_ref, x_ref, u_ref, bias_ref, q_ref, k_ref, v_ref, da_ref, da2_ref, gate_ref, dgated_ref,
-    att_ref, dq_ref, dk_ref, dv_ref, bias_grad_ref, adapter_ref, cells_ref,
+    dall_ref, bias_ref, keep_ref, give_ref,
+    rows_ref, x_ref, u_ref, q_ref, k_ref, v_ref, da_ref, da2_ref, gate_ref, dgated_ref,
+    att_ref, dq_ref, dk_ref, dv_ref, gathered_ref, adapter_ref,
     *, own, heads,
 ):
     peers = recv_ref.shape[0]
@@ -137,23 +156,25 @@
         for place in range(own):
             target[place * count : (place + 1) * count] = half(rows_ref[pl.ds(place, count, stride=own)])
     gathered = recv_ref[:, 2 * cell_rows :].astype(jnp.float32)
-    bias_grad_ref[...] = gathered.reshape(count * bias_rows, lanes)
+    gathered_ref[...] = gathered.reshape(count * bias_rows, lanes)
     for part in range(bias_rows):
-        bias_ref[:, part * lanes : (part + 1) * lanes] = bias_grad_ref[pl.ds(part, count, stride=bias_rows)]
-
-    weights = [weight_ref[index] for index in range(4)]
-    downs = [down_ref[index] for index in range(4)]
-    ups = [up_ref[index] for index in range(4)]
+        bias_ref[:, part * lanes : (part + 1) * lanes] = gathered_ref[pl.ds(part, count, stride=bias_rows)]
+
+    downs = stacked(down_ref, 3)
+    ups = blocked(up_ref, 3)
 
     def project(step):
         rows = pl.ds(pl.multiple_of(step * block, block), block)
         x = x_ref[rows]
         u = u_ref[rows]
-        for index, target in enumerate((q_ref, k_ref, v_ref)):
-            low = half(nt(x, downs[index]))
-            target[rows] = half(nn(x, weights[index]) + nn(low, ups[index]))
-        gate = jax.nn.sigmoid(nn(x, weights[3]))
-        dgated = nt(u, out_weight_ref[...]) + nn(half(nt(u, ups[3])), downs[3])
+        update = nn(half(nt(x, downs)), ups)
+        pair01 = nn(x, beside(weight_ref, 0))
+        pair23 = nn(x, beside(weight_ref, 2))
+        q_ref[rows] = half(pair01[:, :channels] + update[:, :channels])
+        k_ref[rows] = half(pair01[:, channels:] + update[:, channels : 2 * channels])
+        v_ref[rows] = half(pair23[:, :channels] + update[:, 2 * channels :])
+        gate = jax.nn.sigmoid(pair23[:, channels:])
+        dgated = nt(u, out_weight_ref[...]) + nn(half(nt(u, up_ref[3])), down_ref[3])
         gate_ref[rows] = gate
         dgated_ref[rows] = dgated
         dattended = dgated * gate
@@ -181,32 +202,34 @@
             return sum(values[head * joint : (head + 1) * joint] * spots[head] for head in range(joint_heads))
 
         q_wide = spread(q_ref[queries])
-        da_wide = spread(da_ref[queries])
-        da2_wide = spread(da2_ref[queries])
+        da_wide = jnp.concatenate([spread(da_ref[queries]), spread(da2_ref[queries])], axis=1)
         k_all = k_ref[keys]
         v_all = v_ref[keys]
         bias = bias_ref[:, pl.ds(column, block)]
         valid = bias > -1e38
         scores = jnp.where(valid, nt(k_all, q_wide) * scale + bias, -1000000000.0)
         powers = jnp.exp(scores - jnp.max(scores, axis=0, keepdims=True))
-        chances = powers / jnp.sum(powers, axis=0, keepdims=True)
+        chances = powers * (1.0 / jnp.sum(powers, axis=0, keepdims=True))
         rounded = half(chances)
-        dchances = half(nt(v_all, da_wide) + nt(v_all, da2_wide)).astype(jnp.float32)
+        dchances = half(nt(jnp.concatenate([v_all, v_all], axis=1), da_wide)).astype(jnp.float32)
         inner = dchances * chances
         dscores = inner - chances * jnp.sum(inner, axis=0, keepdims=True)
         dscores = jnp.where(valid, dscores, 0.0)
-        scaled = half(dscores * scale)
-        rest = half(dscores * scale - scaled.astype(jnp.float32))
+        scaled = dscores * scale
+        leading = half(scaled)
+        both = jnp.concatenate([leading, half(scaled - leading.astype(jnp.float32))], axis=0)
+        dk = nn(both, q_wide)
+        dv = nn(rounded, da_wide)
         return (
-            queries, keys, column,
-            collect(tn(rounded, v_all)), collect(tn(scaled, k_all) + tn(rest, k_all)),
-            nn(scaled, q_wide) + nn(rest, q_wide), nn(rounded, da_wide) + nn(rounded, da2_wide), dscores,
+            queries, keys,
+            collect(tn(rounded, v_all)), collect(tn(both, jnp.concatenate([k_all, k_all], axis=0))),
+            dk[:count] + dk[count:], dv[:, :channels] + dv[:, channels:], dscores,
         )
 
     if blocks == 1:
         bias_grad = None
         for row in range(own):
-            queries, keys, column, att, dq, dk, dv, dscores = attend(row, 0)
+            queries, keys, att, dq, dk, dv, dscores = attend(row, 0)
             att_ref[queries] = att
             dq_ref[queries] = dq
             dk_ref[keys] = dk
@@ -214,13 +237,12 @@
             bias_grad = dscores if bias_grad is None else bias_grad + dscores
         bias_ref[...] = bias_grad
     else:
-        bias_sum_ref = bias_grad_ref
         for ref in (att_ref, dq_ref, dk_ref, dv_ref):
             ref[...] = jnp.zeros_like(ref)
 
         def each(part):
             def each_row(row, bias_grad):
-                queries, keys, column, att, dq, dk, dv, dscores = attend(row, part)
+                queries, keys, att, dq, dk, dv, dscores = attend(row, part)
                 att_ref[queries] += att
                 dq_ref[queries] += dq
                 dk_ref[keys] += dk
@@ -231,10 +253,10 @@
             bias_ref[:, pl.ds(pl.multiple_of(part * block, block), block)] = bias_grad
 
         repeat(blocks, each)
-    for part in range(bias_rows):
-        bias_grad_ref[pl.ds(part, count, stride=bias_rows)] = bias_ref[:, part * lanes : (part + 1) * lanes]
-
-    adapter_ref[...] = jnp.zeros_like(adapter_ref)
+
+    many = total > block
+    if many:
+        adapter_ref[...] = jnp.zeros_like(adapter_ref)
 
     def finish(step):
         rows = pl.ds(pl.multiple_of(step * block, block), block)
@@ -242,38 +264,61 @@
         u = u_ref[rows]
         att = att_ref[rows]
         gate = gate_ref[rows]
-        dgated = dgated_ref[rows]
         gated = half(gate * att)
-        dgate = half(dgated * att * (gate * (1.0 - gate)))
-        low_out = half(nt(downs[3], gated))
-        dlow_out = half(nt(ups[3], u))
-        downs_grad = [None] * 3 + [nn(dlow_out, gated)]
-        ups_grad = [None] * 3 + [nn(low_out, u)]
-        grad = nt(dgate, weights[3])
-        for index, source in enumerate((dq_ref, dk_ref, dv_ref)):
-            dproj = half(source[rows])
-            ups_grad[index] = nn(half(nt(downs[index], x)), dproj)
-            downs_grad[index] = nn(half(nt(ups[index], dproj)), x)
-            grad = grad + nt(dproj, weights[index]) + nn(half(nt(dproj, ups[index])), downs[index])
-        for index in range(4):
-            adapter_ref[index * rank : (index + 1) * rank] += downs_grad[index]
-            adapter_ref[(4 + index) * rank : (5 + index) * rank] += ups_grad[index]
-        rows_ref[rows] = grad
+        dgate = half(dgated_ref[rows] * att * (gate * (1.0 - gate)))
+        dproj = [half(ref[rows]) for ref in (dq_ref, dk_ref, dv_ref)]
+        dprojs = jnp.concatenate(dproj, axis=1)
+        dall_ref[rows, : 3 * channels] = dprojs
+        dall_ref[rows, 3 * channels :] = dgate
+        low = half(nt(downs, x))
+        dlow = half(nt(ups, dprojs))
+        grads = [
+            nn(dlow, x),
+            nn(half(nt(up_ref[3], u)), gated),
+            *[nn(low[index * rank : (index + 1) * rank], dproj[index]) for index in range(3)],
+            nn(half(nt(down_ref[3], gated)), u),
+        ]
+        grads = jnp.concatenate(grads, axis=0)
+        adapter_ref[...] = adapter_ref[...] + grads if many else grads
 
     repeat(total // block, finish)
 
-    bias_chunk = own * bias_rows
+    side = lax.rem(lax.axis_index("sub"), 2) == 0
+    split = adapter_ref.shape[0] // 2
+    keep_ref[...] = jnp.where(side, adapter_ref[:split], adapter_ref[split:])
+    give_ref[...] = jnp.where(side, adapter_ref[split:], adapter_ref[:split])
+
+
+def cells_kernel(
+    dall_ref, bias_ref, weight_ref, down_ref, up_ref, send_ref, rows_ref, cells_ref, bias_rows_ref, *, own
+):
+    peers = send_ref.shape[0]
+    channels = send_ref.shape[2]
+    count = own * peers
+    cell_rows = own * own
+    total = own * count
+    bias_rows = bias_ref.shape[1] // lanes
+    downs = stacked(down_ref, 3)
+    ups = blocked(up_ref, 3)
+
+    def rows_of(step):
+        rows = pl.ds(pl.multiple_of(step * block, block), block)
+        rows_ref[rows] = (
+            nt(dall_ref[rows, : 2 * channels], beside(weight_ref, 0))
+            + nt(dall_ref[rows, 2 * channels :], beside(weight_ref, 2))
+            + nn(half(nt(dall_ref[rows, : 3 * channels], ups)), downs)
+        )
+
+    repeat(total // block, rows_of)
     for row in range(own):
         for place in range(own):
             cells_ref[pl.ds(row * own + place, peers, stride=cell_rows)] = rows_ref[
                 pl.ds(place * count + row, peers, stride=own)
             ]
+    for part in range(bias_rows):
+        bias_rows_ref[pl.ds(part, count, stride=bias_rows)] = bias_ref[:, part * lanes : (part + 1) * lanes]
     send_ref[:, 0:cell_rows] = half(cells_ref[...]).reshape(peers, cell_rows, channels)
-    send_ref[:, cell_rows:] = half(bias_grad_ref[...]).reshape(peers, bias_chunk, lanes)
-    side = lax.rem(lax.axis_index("sub"), 2) == 0
-    split = adapter_ref.shape[0] // 2
-    keep_ref[...] = jnp.where(side, adapter_ref[:split], adapter_ref[split:])
-    give_ref[...] = jnp.where(side, adapter_ref[split:], adapter_ref[:split])
+    send_ref[:, cell_rows:] = half(bias_rows_ref[...]).reshape(peers, own * bias_rows, lanes)
 
 
 def pack_kernel(cells_ref, keep_ref, taken_ref, send_ref):
@@ -295,15 +340,7 @@
         out_ref[side * quarter : (side + 1) * quarter] = total
 
 
-def after_kernel(
-    recv_ref, mine_ref, theirs_ref, unit_ref, inverse_ref, gain_ref, bias_weight_ref,
-    out_ref, down_ref, up_ref, rows_ref, cells_ref, bias_ref,
-):
-    own, count, channels = out_ref.shape
-    peers = count // own
-    heads = bias_weight_ref.shape[0]
-    cell_rows = own * own
-    bias_rows = heads * count // lanes
+def final_kernel(mine_ref, theirs_ref, down_ref, up_ref):
     side = lax.rem(lax.axis_index("sub"), 2) == 0
     quarter = mine_ref.shape[0] // 2
     for index, ref in enumerate((down_ref, up_ref)):
@@ -311,6 +348,16 @@
         theirs = theirs_ref[index * quarter : (index + 1) * quarter]
         ref[:quarter] = jnp.where(side, mine, theirs)
         ref[quarter:] = jnp.where(side, theirs, mine)
+
+
+def after_kernel(
+    recv_ref, unit_ref, inverse_ref, gain_ref, bias_weight_ref, out_ref, rows_ref, cells_ref, bias_ref
+):
+    own, count, channels = out_ref.shape
+    peers = count // own
+    heads = bias_weight_ref.shape[0]
+    cell_rows = own * own
+    bias_rows = heads * count // lanes
     cells_ref[...] = recv_ref[:, :cell_rows].astype(jnp.float32).reshape(own * count, channels)
     for row in range(own):
         for place in range(own):
@@ -417,29 +464,43 @@
         )
     )
     first_recv = exchange(first_send)
-    cells, keep, give = pl.pallas_call(
+    dall, bias_grad, keep, give = pl.pallas_call(
         functools.partial(middle_kernel, own=own, heads=heads),
         out_shape=(
-            jax.ShapeDtypeStruct((peers, cell_rows + bias_chunk, channels), bf16),
+            jax.ShapeDtypeStruct((total, 4 * channels), bf16),
+            jax.ShapeDtypeStruct((count, heads * count), f32),
             jax.ShapeDtypeStruct((adapter_rows // 2, channels), f32),
             jax.ShapeDtypeStruct((adapter_rows // 2, channels), f32),
         ),
         in_specs=[vmem] * 5,
-        out_specs=(vmem,) * 3,
+        out_specs=(vmem,) * 4,
         scratch_shapes=[
             pltpu.VMEM((total, channels), f32),
-            pltpu.VMEM((total, channels), bf16),
-            pltpu.VMEM((total, channels), bf16),
-            pltpu.VMEM((count, heads * count), f32),
-            *[pltpu.VMEM((total, channels), bf16)] * 5,
+            *[pltpu.VMEM((total, channels), bf16)] * 7,
             *[pltpu.VMEM((total, channels), f32)] * 6,
             pltpu.VMEM((count * bias_rows, lanes), f32),
             pltpu.VMEM((adapter_rows, channels), f32),
-            pltpu.VMEM((total, channels), f32),
         ],
         compiler_params=params,
         name="middle",
     )(first_recv, projection_weight, output_weight, downs, adapter_up_maps)
+    taken = swap_cores(give)
+    cells = pl.pallas_call(
+        functools.partial(cells_kernel, own=own),
+        out_shape=jax.ShapeDtypeStruct((peers, cell_rows + bias_chunk, channels), bf16),
+        in_specs=[vmem] * 5,
+        out_specs=vmem,
+        scratch_shapes=[
+            pltpu.VMEM((total, channels), f32),
+            pltpu.VMEM((total, channels), f32),
+            pltpu.VMEM((count * bias_rows, lanes), f32),
+        ],
+        compiler_params=params,
+        cost_estimate=pl.CostEstimate(
+            flops=10 * total * channels * channels, bytes_accessed=40 * total * channels, transcendentals=0
+        ),
+        name="cells",
+    )(dall, bias_grad, projection_weight, downs, adapter_up_maps)
     second_send = pl.pallas_call(
         pack_kernel,
         out_shape=jax.ShapeDtypeStruct((peers, cell_rows + bias_chunk + adapter_chunk, channels), bf16),
@@ -447,7 +508,7 @@
         out_specs=vmem,
         compiler_params=params,
         name="pack",
-    )(cells, keep, swap_cores(give))
+    )(cells, keep, taken)
     second_recv = exchange(second_send)
     mine = pl.pallas_call(
         functools.partial(adapter_kernel, offset=cell_rows + bias_chunk),
@@ -457,23 +518,31 @@
         compiler_params=params,
         name="adapters",
     )(second_recv)
-    pair_grad, down_grad, up_grad = pl.pallas_call(
+    theirs = swap_cores(mine)
+    pair_grad = pl.pallas_call(
         after_kernel,
-        out_shape=(
-            jax.ShapeDtypeStruct((own, count, channels), bf16),
-            jax.ShapeDtypeStruct((adapter_rows // 2, channels), f32),
-            jax.ShapeDtypeStruct((adapter_rows // 2, channels), f32),
-        ),
-        in_specs=[vmem] * 7,
-        out_specs=(vmem,) * 3,
+        out_shape=jax.ShapeDtypeStruct((own, count, channels), bf16),
+        in_specs=[vmem] * 5,
+        out_specs=vmem,
         scratch_shapes=[
             pltpu.VMEM((total, channels), f32),
             pltpu.VMEM((total, channels), f32),
             pltpu.VMEM((bias_chunk, lanes), f32),
         ],
         compiler_params=params,
+        cost_estimate=pl.CostEstimate(
+            flops=20 * total * channels, bytes_accessed=20 * total * channels, transcendentals=0
+        ),
         name="after",
-    )(second_recv, mine, swap_cores(mine), unit, inverse, gain_kept, bias_weight_kept)
+    )(second_recv, unit, inverse, gain_kept, bias_weight_kept)
+    down_grad, up_grad = pl.pallas_call(
+        final_kernel,
+        out_shape=(jax.ShapeDtypeStruct((adapter_rows // 2, channels), f32),) * 2,
+        in_specs=[vmem] * 2,
+        out_specs=(vmem,) * 2,
+        compiler_params=params,
+        name="final",
+    )(mine, theirs)
     return (
         pair_grad,
         jnp.swapaxes(down_grad.reshape(4, rank, channels), 1, 2),

time: 37.3 us -> 35.9 us (0.962)
  waiting for transfers between devices: 2.39 us -> 0.9 us
    ppermute x2, waiting for transfers between devices: 2.39 us -> 0.9 us  [swap_cores(): lax.ppermute(values, 'sub', [(place, place ^ 1) for place in range(size)])]
    pallas_call x1 -> x3, Pallas kernels: 1.08 us -> 2.12 us  [the longest x1 1.08 us: local(): pl.pallas_call(after_kernel, out_shape=jax.ShapeDtypeStruct((own, count,...]
    pallas_call x1, Pallas kernels: 3.26 us -> 2.33 us  [local(): pl.pallas_call(functools.partial(middle_kernel, own=own, heads=heads), ou...]
  transfers between devices with their start and end apart: 2 -> 2, of which waited for: 2 -> 2; matrix products, arithmetic and copies ran while one was open for 0% -> 0% of each run, Pallas kernels for 0% -> 4%
where the time goes in v4:
time: 35.9 us; the launch traced here: 35.7 us
  blocking collectives  27.9 us (78%)
  Pallas kernels  6.05 us (17%)
  waiting for transfers between devices  0.9 us (3%)
  between operations  0.72 us (2%)
    all_to_all x2, blocking collectives, exchange(): lax.all_to_all(values, group_axes, split_axis=0, concat_axis=0, tiled=True)  27.9 us
    pallas_call x1, Pallas kernels, local(): pl.pallas_call(functools.partial(middle_kernel, own=own, heads=heads), ou...  2.33 us
    pallas_call x1, Pallas kernels, local(): pl.pallas_call(before_kernel, out_shape=(jax.ShapeDtypeStruct((peers, 2 *...  1.57 us
    pallas_call x1, Pallas kernels, local(): pl.pallas_call(after_kernel, out_shape=jax.ShapeDtypeStruct((own, count,...  1.08 us
    ppermute x2, waiting for transfers between devices, swap_cores(): lax.ppermute(values, 'sub', [(place, place ^ 1) for place in range(size)])  0.9 us
  transfers between devices with their start and end apart: 2, of which 2 were waited for; matrix products, arithmetic and copies ran while one was open for 0% of the time, Pallas kernels for 4%

profile of v4, /device:TPU:0, one launch (start us, length us, event | category | flops | bytes accessed | tf_op | source)
XLA Modules:
  0.0 35.7 jit_solution(18115185051752447465)
XLA Ops:
  0.6 1.6 %before.1 = (bf16[16,40,128]{2,1,0:T(8,128)(2,1)S(1)}, f32[256,128]{1,0:T(8,128)S(1)}, f32[256,1]{1,0:T(8,128)S(1)}, f32[1,128]{1,0:T(1,128)S(1)}, bf16[4,128]{1,0:T(4,128)(2,1)S(1)}) custom-call(s32[64]{0:T(128)} %mask_hbm.1, s32[64]{0:T(128)} %label_hbm.1, s32[1,64]{1,0:T(1,128)} %bitcast.10, bf16[4,64,128]{2,1,0:T(8,128)(2,1)} %pair_hbm.1, ...), custom_call_target="tpu_custom_call" | custom-call | tf_op jit(solution)/shard_map/before/pallas_call | solution.py:432
  2.2 0.0 copy-start
  2.2 0.0 copy-start.1
  2.2 0.0 copy-start.2
  2.2 0.0 copy-start.3
  2.3 15.8 %all_to_all.10.recv_ref = bf16[16,40,128]{2,1,0:T(8,128)(2,1)S(1)} all-to-all(bf16[16,40,128]{2,1,0:T(8,128)(2,1)S(1)} %get-tuple-element.14), channel_id=1, replica_groups=mesh['groups'=2,'dap'=4,'sub'=4] {'dap','sub'}, dimensions={0} | all-to-all | bytes 327680 | tf_op jit(solution)/shard_map/all_to_all | solution.py:400
  18.0 0.0 copy-done
  18.0 0.0 copy-done.1
  18.0 0.0 copy-done.2
  18.0 0.0 copy-done.3
  18.0 2.3 %middle.1 = (bf16[256,512]{1,0:T(8,128)(2,1)S(1)}, f32[64,256]{1,0:T(8,128)S(1)}, f32[64,128]{1,0:T(8,128)S(1)}, f32[64,128]{1,0:T(8,128)S(1)}) custom-call(bf16[16,40,128]{2,1,0:T(8,128)(2,1)S(1)} %all_to_all.10.recv_ref, bf16[4,128,128]{2,1,0:T(8,128)(2,1)S(1)} %copy-done, bf16[128,128]{1,0:T(8,128)(2,1)S(1)} %copy-done.3, ...), custom_call_target="tpu_custom_call" | custom-call | tf_op jit(solution)/shard_map/middle/pallas_call | solution.py:467
  20.4 0.1 collective-permute-start
  20.4 0.4 %cells.1.cells_ref = bf16[16,24,128]{2,1,0:T(8,128)(2,1)S(1)} custom-call(bf16[256,512]{1,0:T(8,128)(2,1)S(1)} %get-tuple-element.15.dall_ref, f32[64,256]{1,0:T(8,128)S(1)} %get-tuple-element.16.bias_ref, bf16[4,128,128]{2,1,0:T(8,128)(2,1)S(1)} %copy-done, bf16[4,16,128]{2,1,0:T(8,128)(2,1)S(1)} %bitcast.9, bf16[4,16,128]{2,1,0:T(8,128)(2,1)S(1)} %copy-done.2), custom_call_target="tpu_custom_call" | custom-call | flops 41943040 | bytes 1310720 | tf_op jit(solution)/shard_map/cells/pallas_call | solution.py:488
  20.8 0.8 %collective-permute-done.taken_ref = f32[64,128]{1,0:T(8,128)S(1)} collective-permute-done((f32[64,128]{1,0:T(8,128)S(1)}, f32[64,128]{1,0:T(8,128)S(1)}, u32[]{:S(2)}, u32[]{:S(2)}) %collective-permute-start) | collective-permute-done | bytes 32800 | tf_op jit(solution)/shard_map/ppermute | solution.py:396
  21.7 12.1 %all_to_all.11.recv_ref = bf16[16,56,128]{2,1,0:T(8,128)(2,1)S(1)} all-to-all(bf16[16,56,128]{2,1,0:T(8,128)(2,1)S(1)} %pack.1), channel_id=1, replica_groups=mesh['groups'=2,'dap'=4,'sub'=4] {'dap','sub'}, dimensions={0} | all-to-all | bytes 458752 | tf_op jit(solution)/shard_map/all_to_all | solution.py:400
  33.8 0.1 collective-permute-start.1
  33.9 1.1 %after.1 = bf16[4,64,128]{2,1,0:T(8,128)(2,1)} custom-call(bf16[16,56,128]{2,1,0:T(8,128)(2,1)S(1)} %all_to_all.11.recv_ref, f32[256,128]{1,0:T(8,128)S(1)} %get-tuple-element.19.unit_ref, f32[256,1]{1,0:T(8,128)S(1)} %get-tuple-element.20.inverse_ref, f32[1,128]{1,0:T(1,128)S(1)} %get-tuple-element.21.gain_ref, ...), custom_call_target="tpu_custom_call" | custom-call | flops 655360 | bytes 655360 | tf_op jit(solution)/shard_map/after/pallas_call | solution.py:522
  35.0 0.1 collective-permute-done.1.theirs_ref
  35.1 0.6 %final.1 = (f32[64,128]{1,0:T(8,128)}, f32[64,128]{1,0:T(8,128)}) custom-call(f32[64,128]{1,0:T(8,128)S(1)} %adapters.1.mine_ref, f32[64,128]{1,0:T(8,128)S(1)} %collective-permute-done.1.theirs_ref), custom_call_target="tpu_custom_call" | custom-call | tf_op jit(solution)/shard_map/final/pallas_call | solution.py:538
  (2 shorter events, 0.0 us)
Async XLA Ops:
  2.2 15.8 %copy-start = (bf16[4,128,128]{2,1,0:T(8,128)(2,1)S(1)}, bf16[4,128,128]{2,1,0:T(8,128)(2,1)}, u32[]{:S(2)}) copy-start(bf16[4,128,128]{2,1,0:T(8,128)(2,1)} %weight_ref.3) | copy-start | bytes 393220
  2.2 15.8 %copy-start.1 = (bf16[4,128,16]{1,2,0:T(8,128)(2,1)S(1)}, bf16[4,128,16]{1,2,0:T(8,128)(2,1)}, u32[]{:S(2)}) copy-start(bf16[4,128,16]{1,2,0:T(8,128)(2,1)} %param.20) | copy-start | bytes 49156
  2.2 15.8 %copy-start.2 = (bf16[4,16,128]{2,1,0:T(8,128)(2,1)S(1)}, bf16[4,16,128]{2,1,0:T(8,128)(2,1)}, u32[]{:S(2)}) copy-start(bf16[4,16,128]{2,1,0:T(8,128)(2,1)} %up_ref.3) | copy-start | bytes 49156
  2.2 15.8 %copy-start.3 = (bf16[128,128]{1,0:T(8,128)(2,1)S(1)}, bf16[128,128]{1,0:T(8,128)(2,1)}, u32[]{:S(2)}) copy-start(bf16[128,128]{1,0:T(8,128)(2,1)} %out_weight_ref.1) | copy-start | bytes 98308
  20.4 1.3 %collective-permute-start = (f32[64,128]{1,0:T(8,128)S(1)}, f32[64,128]{1,0:T(8,128)S(1)}, u32[]{:S(2)}, u32[]{:S(2)}) collective-permute-start(f32[64,128]{1,0:T(8,128)S(1)} %get-tuple-element.18), channel_id=1, source_target_pairs={{0,1},{1,0},{2,3},{3,2},{4,5},{5,4},{6,7},{7,6},{8,9},{9,8},{10,11... | collective-permute-start | bytes 98312 | tf_op jit(solution)/shard_map/ppermute | solution.py:396
  33.8 1.3 %collective-permute-start.1 = (f32[64,128]{1,0:T(8,128)S(1)}, f32[64,128]{1,0:T(8,128)S(1)}, u32[]{:S(2)}, u32[]{:S(2)}) collective-permute-start(f32[64,128]{1,0:T(8,128)S(1)} %adapters.1.mine_ref), channel_id=1, source_target_pairs={{0,1},{1,0},{2,3},{3,2},{4,5},{5,4},{6,7},{7,6},{8,9},{9,8},{10,11... | collective-permute-start | bytes 98312 | tf_op jit(solution)/shard_map/ppermute | solution.py:396

commit v5 on v4

--- a/solution.py
+++ b/solution.py
@@ -12,6 +12,7 @@
 lanes = 128
 block = 256
 masked_bias = -3e38
+together = 4
 group_axes = ("dap", "sub")
 vmem = pl.BlockSpec(memory_space=pltpu.VMEM)
 hbm = pl.BlockSpec(memory_space=pltpu.HBM)
@@ -54,7 +55,7 @@
     ]
     for copy in copies:
         copy.start()
-    for copy in copies[:-1]:
+    for copy in copies[1:-1]:
         copy.wait()
     own, count, channels = pair_ref.shape
     peers = count // own
@@ -65,6 +66,22 @@
     gain = gain_ref[...]
     key_pos = lax.broadcasted_iota(jnp.int32, (1, count), 1)
     bin_ids = lax.broadcasted_iota(jnp.int32, (bins, count), 0)
+    table = table_ref[...]
+    table_parts = []
+    for _ in range(3):
+        table_parts.append(half(table))
+        table = table - table_parts[-1].astype(jnp.float32)
+    table_parts = jnp.concatenate(table_parts, axis=0)
+
+    def relative_bias(here):
+        same = label_row_ref[...] == label_ref[here]
+        offset = jnp.clip(here - key_pos, -reach, reach) + reach
+        onehot = half((bin_ids == jnp.where(same, offset, bins - 1)).astype(jnp.float32))
+        found = nn(table_parts, onehot)
+        return found[:heads] + found[heads : 2 * heads] + found[2 * heads :]
+
+    relative = [relative_bias(first + row) for row in range(own)]
+    copies[0].wait()
     for row in range(own):
         here = first + row
         values = pair_ref[row].astype(jnp.float32)
@@ -75,14 +92,7 @@
         unit_ref[row * count : (row + 1) * count] = unit
         inverse_ref[row * count : (row + 1) * count] = inverse
         normed_ref[row * count : (row + 1) * count] = normed
-        same = label_row_ref[...] == label_ref[here]
-        offset = jnp.clip(here - key_pos, -reach, reach) + reach
-        onehot = (bin_ids == jnp.where(same, offset, bins - 1)).astype(jnp.float32)
-        relative = lax.dot_general(
-            table_ref[...], onehot, (((1,), (0,)), ((), ())),
-            precision=lax.Precision.HIGHEST, preferred_element_type=jnp.float32,
-        )
-        bias = half(nt(bias_weight_ref[...], half(normed)) + relative).astype(jnp.float32)
+        bias = half(nt(bias_weight_ref[...], half(normed)) + relative[row]).astype(jnp.float32)
         bias = jnp.where(mask_ref[here] > 0, bias, masked_bias)
         for head in range(heads):
             if count < lanes:
@@ -187,53 +197,65 @@
     head_of = lax.broadcasted_iota(jnp.int32, (1, channels), 1) // width
     blocks = heads * count // block
 
-    def attend(row, part):
+    def attend(rows, part):
         start = part * block // count
         column = pl.multiple_of(part * block, block)
         first = 0 if count <= block else pl.multiple_of(lax.rem(part * block, count), block)
-        queries = pl.ds(row * count + first, joint)
-        keys = pl.ds(row * count, count)
+        queries = [pl.ds(row * count + first, joint) for row in rows]
+        keys = [pl.ds(row * count, count) for row in rows]
         spots = [(head_of == start + head).astype(jnp.float32) for head in range(joint_heads)]
+        marks = [half(spot) for spot in spots]
 
         def spread(values):
-            return jnp.concatenate([values * half(spot) for spot in spots], axis=0)
+            return jnp.concatenate([values * mark for mark in marks], axis=0)
 
         def collect(values):
             return sum(values[head * joint : (head + 1) * joint] * spots[head] for head in range(joint_heads))
 
-        q_wide = spread(q_ref[queries])
-        da_wide = jnp.concatenate([spread(da_ref[queries]), spread(da2_ref[queries])], axis=1)
-        k_all = k_ref[keys]
-        v_all = v_ref[keys]
         bias = bias_ref[:, pl.ds(column, block)]
         valid = bias > -1e38
-        scores = jnp.where(valid, nt(k_all, q_wide) * scale + bias, -1000000000.0)
-        powers = jnp.exp(scores - jnp.max(scores, axis=0, keepdims=True))
-        chances = powers * (1.0 / jnp.sum(powers, axis=0, keepdims=True))
-        rounded = half(chances)
-        dchances = half(nt(jnp.concatenate([v_all, v_all], axis=1), da_wide)).astype(jnp.float32)
-        inner = dchances * chances
-        dscores = inner - chances * jnp.sum(inner, axis=0, keepdims=True)
-        dscores = jnp.where(valid, dscores, 0.0)
-        scaled = dscores * scale
-        leading = half(scaled)
-        both = jnp.concatenate([leading, half(scaled - leading.astype(jnp.float32))], axis=0)
-        dk = nn(both, q_wide)
-        dv = nn(rounded, da_wide)
-        return (
-            queries, keys,
-            collect(tn(rounded, v_all)), collect(tn(both, jnp.concatenate([k_all, k_all], axis=0))),
-            dk[:count] + dk[count:], dv[:, :channels] + dv[:, channels:], dscores,
-        )
+        q_wide = [spread(q_ref[at]) for at in queries]
+        da_wide = [jnp.concatenate([spread(da_ref[at]), spread(da2_ref[at])], axis=1) for at in queries]
+        k_all = [k_ref[at] for at in keys]
+        v_all = [v_ref[at] for at in keys]
+        scores = [
+            jnp.where(valid, nt(key, query) * scale + bias, -1000000000.0) for key, query in zip(k_all, q_wide)
+        ]
+        dchances = [
+            half(nt(jnp.concatenate([value, value], axis=1), da)).astype(jnp.float32)
+            for value, da in zip(v_all, da_wide)
+        ]
+        powers = [jnp.exp(each - jnp.max(each, axis=0, keepdims=True)) for each in scores]
+        chances = [each * (1.0 / jnp.sum(each, axis=0, keepdims=True)) for each in powers]
+        rounded = [half(each) for each in chances]
+        att = [collect(tn(each, value)) for each, value in zip(rounded, v_all)]
+        dv = [nn(each, da) for each, da in zip(rounded, da_wide)]
+        inner = [left * right for left, right in zip(dchances, chances)]
+        dscores = [
+            jnp.where(valid, left - right * jnp.sum(left, axis=0, keepdims=True), 0.0)
+            for left, right in zip(inner, chances)
+        ]
+        scaled = [each * scale for each in dscores]
+        leading = [half(each) for each in scaled]
+        both = [
+            jnp.concatenate([lead, half(each - lead.astype(jnp.float32))], axis=0)
+            for lead, each in zip(leading, scaled)
+        ]
+        dk = [nn(each, query) for each, query in zip(both, q_wide)]
+        dq = [collect(tn(each, jnp.concatenate([key, key], axis=0))) for each, key in zip(both, k_all)]
+        dk = [each[:count] + each[count:] for each in dk]
+        dv = [each[:, :channels] + each[:, channels:] for each in dv]
+        return list(zip(queries, keys, att, dq, dk, dv)), sum(dscores[1:], dscores[0])
 
     if blocks == 1:
         bias_grad = None
-        for row in range(own):
-            queries, keys, att, dq, dk, dv, dscores = attend(row, 0)
-            att_ref[queries] = att
-            dq_ref[queries] = dq
-            dk_ref[keys] = dk
-            dv_ref[keys] = dv
+        for row in range(0, own, together):
+            results, dscores = attend(range(row, min(row + together, own)), 0)
+            for queries, keys, att, dq, dk, dv in results:
+                att_ref[queries] = att
+                dq_ref[queries] = dq
+                dk_ref[keys] = dk
+                dv_ref[keys] = dv
             bias_grad = dscores if bias_grad is None else bias_grad + dscores
         bias_ref[...] = bias_grad
     else:
@@ -242,7 +264,7 @@
 
         def each(part):
             def each_row(row, bias_grad):
-                queries, keys, att, dq, dk, dv, dscores = attend(row, part)
+                ((queries, keys, att, dq, dk, dv),), dscores = attend([row], part)
                 att_ref[queries] += att
                 dq_ref[queries] += dq
                 dk_ref[keys] += dk

time: 35.9 us -> 35.4 us (0.986)
  Pallas kernels: 6.05 us -> 5.54 us
    pallas_call x1, Pallas kernels: 2.33 us -> 1.84 us  [local(): pl.pallas_call(functools.partial(middle_kernel, own=own, heads=heads), ou...]
where the time goes in v5:
time: 35.4 us; the launch traced here: 35.1 us
  blocking collectives  27.9 us (79%)
  Pallas kernels  5.54 us (16%)
  waiting for transfers between devices  0.91 us (3%)
  between operations  0.71 us (2%)
    all_to_all x2, blocking collectives, exchange(): lax.all_to_all(values, group_axes, split_axis=0, concat_axis=0, tiled=True)  27.9 us
    pallas_call x1, Pallas kernels, local(): pl.pallas_call(functools.partial(middle_kernel, own=own, heads=heads), ou...  1.84 us
    pallas_call x1, Pallas kernels, local(): pl.pallas_call(before_kernel, out_shape=(jax.ShapeDtypeStruct((peers, 2 *...  1.51 us
    pallas_call x1, Pallas kernels, local(): pl.pallas_call(after_kernel, out_shape=jax.ShapeDtypeStruct((own, count,...  1.08 us
    ppermute x2, waiting for transfers between devices, swap_cores(): lax.ppermute(values, 'sub', [(place, place ^ 1) for place in range(size)])  0.91 us
  transfers between devices with their start and end apart: 2, of which 2 were waited for; matrix products, arithmetic and copies ran while one was open for 0% of the time, Pallas kernels for 4%

profile of v5, /device:TPU:0, one launch (start us, length us, event | category | flops | bytes accessed | tf_op | source)
XLA Modules:
  0.0 35.1 jit_solution(17324025542923630193)
XLA Ops:
  0.6 1.5 %before.1 = (bf16[16,40,128]{2,1,0:T(8,128)(2,1)S(1)}, f32[256,128]{1,0:T(8,128)S(1)}, f32[256,1]{1,0:T(8,128)S(1)}, f32[1,128]{1,0:T(1,128)S(1)}, bf16[4,128]{1,0:T(4,128)(2,1)S(1)}) custom-call(s32[64]{0:T(128)} %mask_hbm.1, s32[64]{0:T(128)} %label_hbm.1, s32[1,64]{1,0:T(1,128)} %bitcast.10, bf16[4,64,128]{2,1,0:T(8,128)(2,1)} %pair_hbm.1, ...), custom_call_target="tpu_custom_call" | custom-call | tf_op jit(solution)/shard_map/before/pallas_call | solution.py:454
  2.1 0.0 copy-start
  2.2 0.0 copy-start.1
  2.2 0.0 copy-start.2
  2.2 0.0 copy-start.3
  2.2 15.8 %all_to_all.10.recv_ref = bf16[16,40,128]{2,1,0:T(8,128)(2,1)S(1)} all-to-all(bf16[16,40,128]{2,1,0:T(8,128)(2,1)S(1)} %get-tuple-element.14), channel_id=1, replica_groups=mesh['groups'=2,'dap'=4,'sub'=4] {'dap','sub'}, dimensions={0} | all-to-all | bytes 327680 | tf_op jit(solution)/shard_map/all_to_all | solution.py:422
  17.9 0.0 copy-done
  18.0 0.0 copy-done.1
  18.0 0.0 copy-done.2
  18.0 0.0 copy-done.3
  18.0 1.8 %middle.1 = (bf16[256,512]{1,0:T(8,128)(2,1)S(1)}, f32[64,256]{1,0:T(8,128)S(1)}, f32[64,128]{1,0:T(8,128)S(1)}, f32[64,128]{1,0:T(8,128)S(1)}) custom-call(bf16[16,40,128]{2,1,0:T(8,128)(2,1)S(1)} %all_to_all.10.recv_ref, bf16[4,128,128]{2,1,0:T(8,128)(2,1)S(1)} %copy-done, bf16[128,128]{1,0:T(8,128)(2,1)S(1)} %copy-done.3, ...), custom_call_target="tpu_custom_call" | custom-call | tf_op jit(solution)/shard_map/middle/pallas_call | solution.py:489
  19.8 0.0 collective-permute-start
  19.8 0.4 %cells.1.cells_ref = bf16[16,24,128]{2,1,0:T(8,128)(2,1)S(1)} custom-call(bf16[256,512]{1,0:T(8,128)(2,1)S(1)} %get-tuple-element.15.dall_ref, f32[64,256]{1,0:T(8,128)S(1)} %get-tuple-element.16.bias_ref, bf16[4,128,128]{2,1,0:T(8,128)(2,1)S(1)} %copy-done, bf16[4,16,128]{2,1,0:T(8,128)(2,1)S(1)} %bitcast.9, bf16[4,16,128]{2,1,0:T(8,128)(2,1)S(1)} %copy-done.2), custom_call_target="tpu_custom_call" | custom-call | flops 41943040 | bytes 1310720 | tf_op jit(solution)/shard_map/cells/pallas_call | solution.py:510
  20.3 0.8 %collective-permute-done.taken_ref = f32[64,128]{1,0:T(8,128)S(1)} collective-permute-done((f32[64,128]{1,0:T(8,128)S(1)}, f32[64,128]{1,0:T(8,128)S(1)}, u32[]{:S(2)}, u32[]{:S(2)}) %collective-permute-start) | collective-permute-done | bytes 32800 | tf_op jit(solution)/shard_map/ppermute | solution.py:418
  21.1 12.1 %all_to_all.11.recv_ref = bf16[16,56,128]{2,1,0:T(8,128)(2,1)S(1)} all-to-all(bf16[16,56,128]{2,1,0:T(8,128)(2,1)S(1)} %pack.1), channel_id=1, replica_groups=mesh['groups'=2,'dap'=4,'sub'=4] {'dap','sub'}, dimensions={0} | all-to-all | bytes 458752 | tf_op jit(solution)/shard_map/all_to_all | solution.py:422
  33.2 0.1 collective-permute-start.1
  33.3 1.1 %after.1 = bf16[4,64,128]{2,1,0:T(8,128)(2,1)} custom-call(bf16[16,56,128]{2,1,0:T(8,128)(2,1)S(1)} %all_to_all.11.recv_ref, f32[256,128]{1,0:T(8,128)S(1)} %get-tuple-element.19.unit_ref, f32[256,1]{1,0:T(8,128)S(1)} %get-tuple-element.20.inverse_ref, f32[1,128]{1,0:T(1,128)S(1)} %get-tuple-element.21.gain_ref, ...), custom_call_target="tpu_custom_call" | custom-call | flops 655360 | bytes 655360 | tf_op jit(solution)/shard_map/after/pallas_call | solution.py:544
  34.4 0.1 collective-permute-done.1.theirs_ref
  34.5 0.6 %final.1 = (f32[64,128]{1,0:T(8,128)}, f32[64,128]{1,0:T(8,128)}) custom-call(f32[64,128]{1,0:T(8,128)S(1)} %adapters.1.mine_ref, f32[64,128]{1,0:T(8,128)S(1)} %collective-permute-done.1.theirs_ref), custom_call_target="tpu_custom_call" | custom-call | tf_op jit(solution)/shard_map/final/pallas_call | solution.py:560
  (2 shorter events, 0.0 us)
Async XLA Ops:
  2.1 15.8 %copy-start = (bf16[4,128,128]{2,1,0:T(8,128)(2,1)S(1)}, bf16[4,128,128]{2,1,0:T(8,128)(2,1)}, u32[]{:S(2)}) copy-start(bf16[4,128,128]{2,1,0:T(8,128)(2,1)} %weight_ref.3) | copy-start | bytes 393220
  2.2 15.8 %copy-start.1 = (bf16[4,128,16]{1,2,0:T(8,128)(2,1)S(1)}, bf16[4,128,16]{1,2,0:T(8,128)(2,1)}, u32[]{:S(2)}) copy-start(bf16[4,128,16]{1,2,0:T(8,128)(2,1)} %param.20) | copy-start | bytes 49156
  2.2 15.8 %copy-start.2 = (bf16[4,16,128]{2,1,0:T(8,128)(2,1)S(1)}, bf16[4,16,128]{2,1,0:T(8,128)(2,1)}, u32[]{:S(2)}) copy-start(bf16[4,16,128]{2,1,0:T(8,128)(2,1)} %up_ref.3) | copy-start | bytes 49156
  2.2 15.8 %copy-start.3 = (bf16[128,128]{1,0:T(8,128)(2,1)S(1)}, bf16[128,128]{1,0:T(8,128)(2,1)}, u32[]{:S(2)}) copy-start(bf16[128,128]{1,0:T(8,128)(2,1)} %out_weight_ref.1) | copy-start | bytes 98308
  19.8 1.2 %collective-permute-start = (f32[64,128]{1,0:T(8,128)S(1)}, f32[64,128]{1,0:T(8,128)S(1)}, u32[]{:S(2)}, u32[]{:S(2)}) collective-permute-start(f32[64,128]{1,0:T(8,128)S(1)} %get-tuple-element.18), channel_id=1, source_target_pairs={{0,1},{1,0},{2,3},{3,2},{4,5},{5,4},{6,7},{7,6},{8,9},{9,8},{10,11... | collective-permute-start | bytes 98312 | tf_op jit(solution)/shard_map/ppermute | solution.py:418
  33.2 1.3 %collective-permute-start.1 = (f32[64,128]{1,0:T(8,128)S(1)}, f32[64,128]{1,0:T(8,128)S(1)}, u32[]{:S(2)}, u32[]{:S(2)}) collective-permute-start(f32[64,128]{1,0:T(8,128)S(1)} %adapters.1.mine_ref), channel_id=1, source_target_pairs={{0,1},{1,0},{2,3},{3,2},{4,5},{5,4},{6,7},{7,6},{8,9},{9,8},{10,11... | collective-permute-start | bytes 98312 | tf_op jit(solution)/shard_map/ppermute | solution.py:418

commit v6 on v5

--- a/solution.py
+++ b/solution.py
@@ -142,11 +142,49 @@
     return jnp.concatenate([weight_ref[first], weight_ref[first + 1]], axis=1)
 
 
+def adapter_half(given, target_ref, x_ref, u_ref, gate_ref, att_ref, dprojs_ref, down_ref, up_ref):
+    total, channels = x_ref.shape
+    rank = down_ref.shape[1]
+    steps = total // block
+    first = lax.rem(lax.axis_index("sub"), 2) == 0
+    if steps > 1:
+        target_ref[...] = jnp.zeros_like(target_ref)
+
+    def upper(x, u, gated, dprojs):
+        low = half(nt(stacked(down_ref, 3), x))
+        return [
+            *[
+                nn(low[index * rank : (index + 1) * rank], dprojs[:, index * channels : (index + 1) * channels])
+                for index in range(3)
+            ],
+            nn(half(nt(down_ref[3], gated)), u),
+        ]
+
+    def lower(x, u, gated, dprojs):
+        return [nn(half(nt(blocked(up_ref, 3), dprojs)), x), nn(half(nt(up_ref[3], u)), gated)]
+
+    def step_of(part):
+        def step(index):
+            rows = pl.ds(pl.multiple_of(index * block, block), block)
+            gated = half(gate_ref[rows] * att_ref[rows])
+            found = jnp.concatenate(part(x_ref[rows], u_ref[rows], gated, dprojs_ref[rows]), axis=0)
+            target_ref[...] = target_ref[...] + found if steps > 1 else found
+
+        return step
+
+    @pl.when(first == given)
+    def _():
+        repeat(steps, step_of(upper))
+
+    @pl.when(first != given)
+    def _():
+        repeat(steps, step_of(lower))
+
+
 def middle_kernel(
     recv_ref, weight_ref, out_weight_ref, down_ref, up_ref,
-    dall_ref, bias_ref, keep_ref, give_ref,
-    rows_ref, x_ref, u_ref, q_ref, k_ref, v_ref, da_ref, da2_ref, gate_ref, dgated_ref,
-    att_ref, dq_ref, dk_ref, dv_ref, gathered_ref, adapter_ref,
+    dprojs_ref, x_ref, u_ref, gate_ref, dgated_ref, att_ref, bias_ref, give_ref,
+    rows_ref, q_ref, k_ref, v_ref, da_ref, da2_ref, dq_ref, dk_ref, dv_ref, gathered_ref,
     *, own, heads,
 ):
     peers = recv_ref.shape[0]
@@ -155,7 +193,6 @@
     cell_rows = own * own
     width = channels // heads
     scale = 1.0 / math.sqrt(width)
-    rank = down_ref.shape[1]
     bias_rows = heads * count // lanes
     total = own * count
     joint = min(count, block)
@@ -276,43 +313,18 @@
 
         repeat(blocks, each)
 
-    many = total > block
-    if many:
-        adapter_ref[...] = jnp.zeros_like(adapter_ref)
-
     def finish(step):
         rows = pl.ds(pl.multiple_of(step * block, block), block)
-        x = x_ref[rows]
-        u = u_ref[rows]
-        att = att_ref[rows]
-        gate = gate_ref[rows]
-        gated = half(gate * att)
-        dgate = half(dgated_ref[rows] * att * (gate * (1.0 - gate)))
-        dproj = [half(ref[rows]) for ref in (dq_ref, dk_ref, dv_ref)]
-        dprojs = jnp.concatenate(dproj, axis=1)
-        dall_ref[rows, : 3 * channels] = dprojs
-        dall_ref[rows, 3 * channels :] = dgate
-        low = half(nt(downs, x))
-        dlow = half(nt(ups, dprojs))
-        grads = [
-            nn(dlow, x),
-            nn(half(nt(up_ref[3], u)), gated),
-            *[nn(low[index * rank : (index + 1) * rank], dproj[index]) for index in range(3)],
-            nn(half(nt(down_ref[3], gated)), u),
-        ]
-        grads = jnp.concatenate(grads, axis=0)
-        adapter_ref[...] = adapter_ref[...] + grads if many else grads
+        for index, ref in enumerate((dq_ref, dk_ref, dv_ref)):
+            dprojs_ref[rows, index * channels : (index + 1) * channels] = half(ref[rows])
 
     repeat(total // block, finish)
-
-    side = lax.rem(lax.axis_index("sub"), 2) == 0
-    split = adapter_ref.shape[0] // 2
-    keep_ref[...] = jnp.where(side, adapter_ref[:split], adapter_ref[split:])
-    give_ref[...] = jnp.where(side, adapter_ref[split:], adapter_ref[:split])
+    adapter_half(True, give_ref, x_ref, u_ref, gate_ref, att_ref, dprojs_ref, down_ref, up_ref)
 
 
 def cells_kernel(
-    dall_ref, bias_ref, weight_ref, down_ref, up_ref, send_ref, rows_ref, cells_ref, bias_rows_ref, *, own
+    dprojs_ref, x_ref, u_ref, gate_ref, dgated_ref, att_ref, bias_ref, weight_ref, down_ref, up_ref,
+    send_ref, keep_ref, rows_ref, cells_ref, bias_rows_ref, *, own
 ):
     peers = send_ref.shape[0]
     channels = send_ref.shape[2]
@@ -325,13 +337,17 @@
 
     def rows_of(step):
         rows = pl.ds(pl.multiple_of(step * block, block), block)
+        gate = gate_ref[rows]
+        dgate = half(dgated_ref[rows] * att_ref[rows] * (gate * (1.0 - gate)))
+        dprojs = dprojs_ref[rows]
         rows_ref[rows] = (
-            nt(dall_ref[rows, : 2 * channels], beside(weight_ref, 0))
-            + nt(dall_ref[rows, 2 * channels :], beside(weight_ref, 2))
-            + nn(half(nt(dall_ref[rows, : 3 * channels], ups)), downs)
+            nt(dprojs[:, : 2 * channels], beside(weight_ref, 0))
+            + nt(jnp.concatenate([dprojs[:, 2 * channels :], dgate], axis=1), beside(weight_ref, 2))
+            + nn(half(nt(dprojs, ups)), downs)
         )
 
     repeat(total // block, rows_of)
+    adapter_half(False, keep_ref, x_ref, u_ref, gate_ref, att_ref, dprojs_ref, down_ref, up_ref)
     for row in range(own):
         for place in range(own):
             cells_ref[pl.ds(row * own + place, peers, stride=cell_rows)] = rows_ref[
@@ -486,32 +502,35 @@
         )
     )
     first_recv = exchange(first_send)
-    dall, bias_grad, keep, give = pl.pallas_call(
+    *kept, give = pl.pallas_call(
         functools.partial(middle_kernel, own=own, heads=heads),
         out_shape=(
-            jax.ShapeDtypeStruct((total, 4 * channels), bf16),
+            jax.ShapeDtypeStruct((total, 3 * channels), bf16),
+            *[jax.ShapeDtypeStruct((total, channels), bf16)] * 2,
+            *[jax.ShapeDtypeStruct((total, channels), f32)] * 3,
             jax.ShapeDtypeStruct((count, heads * count), f32),
-            jax.ShapeDtypeStruct((adapter_rows // 2, channels), f32),
             jax.ShapeDtypeStruct((adapter_rows // 2, channels), f32),
         ),
         in_specs=[vmem] * 5,
-        out_specs=(vmem,) * 4,
+        out_specs=(vmem,) * 8,
         scratch_shapes=[
             pltpu.VMEM((total, channels), f32),
-            *[pltpu.VMEM((total, channels), bf16)] * 7,
-            *[pltpu.VMEM((total, channels), f32)] * 6,
+            *[pltpu.VMEM((total, channels), bf16)] * 5,
+            *[pltpu.VMEM((total, channels), f32)] * 3,
             pltpu.VMEM((count * bias_rows, lanes), f32),
-            pltpu.VMEM((adapter_rows, channels), f32),
         ],
         compiler_params=params,
         name="middle",
     )(first_recv, projection_weight, output_weight, downs, adapter_up_maps)
     taken = swap_cores(give)
-    cells = pl.pallas_call(
+    cells, keep = pl.pallas_call(
         functools.partial(cells_kernel, own=own),
-        out_shape=jax.ShapeDtypeStruct((peers, cell_rows + bias_chunk, channels), bf16),
-        in_specs=[vmem] * 5,
-        out_specs=vmem,
+        out_shape=(
+            jax.ShapeDtypeStruct((peers, cell_rows + bias_chunk, channels), bf16),
+            jax.ShapeDtypeStruct((adapter_rows // 2, channels), f32),
+        ),
+        in_specs=[vmem] * 10,
+        out_specs=(vmem,) * 2,
         scratch_shapes=[
             pltpu.VMEM((total, channels), f32),
             pltpu.VMEM((total, channels), f32),
@@ -522,7 +541,7 @@
             flops=10 * total * channels * channels, bytes_accessed=40 * total * channels, transcendentals=0
         ),
         name="cells",
-    )(dall, bias_grad, projection_weight, downs, adapter_up_maps)
+    )(*kept, projection_weight, downs, adapter_up_maps)
     second_send = pl.pallas_call(
         pack_kernel,
         out_shape=jax.ShapeDtypeStruct((peers, cell_rows + bias_chunk + adapter_chunk, channels), bf16),

time: 35.4 us -> 35.1 us (level)
  waiting for transfers between devices: 0.91 us -> 0.45 us
    ppermute x2, waiting for transfers between devices: 0.91 us -> 0.45 us  [swap_cores(): lax.ppermute(values, 'sub', [(place, place ^ 1) for place in range(size)])]
    pallas_call x1, Pallas kernels: 0.43 us -> 0.88 us  [local(): pl.pallas_call(functools.partial(cells_kernel, own=own), out_shape=(jax.S...]
  transfers between devices with their start and end apart: 2 -> 2, of which waited for: 2 -> 2; matrix products, arithmetic and copies ran while one was open for 0% -> 0% of each run, Pallas kernels for 4% -> 6%
where the time goes in v6:
time: 35.1 us; the launch traced here: 34.9 us
  blocking collectives  27.9 us (79%)
  Pallas kernels  5.79 us (16%)
  between operations  0.71 us (2%)
  waiting for transfers between devices  0.45 us (1%)
    all_to_all x2, blocking collectives, exchange(): lax.all_to_all(values, group_axes, split_axis=0, concat_axis=0, tiled=True)  27.9 us
    pallas_call x1, Pallas kernels, local(): pl.pallas_call(functools.partial(middle_kernel, own=own, heads=heads), ou...  1.64 us
    pallas_call x1, Pallas kernels, local(): pl.pallas_call(before_kernel, out_shape=(jax.ShapeDtypeStruct((peers, 2 *...  1.51 us
    pallas_call x1, Pallas kernels, local(): pl.pallas_call(after_kernel, out_shape=jax.ShapeDtypeStruct((own, count,...  1.08 us
    pallas_call x1, Pallas kernels, local(): pl.pallas_call(functools.partial(cells_kernel, own=own), out_shape=(jax.S...  0.88 us
  transfers between devices with their start and end apart: 2, of which 2 were waited for; matrix products, arithmetic and copies ran while one was open for 0% of the time, Pallas kernels for 6%

profile of v6, /device:TPU:0, one launch (start us, length us, event | category | flops | bytes accessed | tf_op | source)
XLA Modules:
  0.0 34.9 jit_solution(14308933840735209652)
XLA Ops:
  0.6 1.5 %before.1 = (bf16[16,40,128]{2,1,0:T(8,128)(2,1)S(1)}, f32[256,128]{1,0:T(8,128)S(1)}, f32[256,1]{1,0:T(8,128)S(1)}, f32[1,128]{1,0:T(1,128)S(1)}, bf16[4,128]{1,0:T(4,128)(2,1)S(1)}) custom-call(s32[64]{0:T(128)} %mask_hbm.1, s32[64]{0:T(128)} %label_hbm.1, s32[1,64]{1,0:T(1,128)} %bitcast.10, bf16[4,64,128]{2,1,0:T(8,128)(2,1)} %pair_hbm.1, ...), custom_call_target="tpu_custom_call" | custom-call | tf_op jit(solution)/shard_map/before/pallas_call | solution.py:470
  2.1 0.0 copy-start
  2.2 0.0 copy-start.1
  2.2 0.0 copy-start.2
  2.2 0.0 copy-start.3
  2.2 15.8 %all_to_all.10.recv_ref = bf16[16,40,128]{2,1,0:T(8,128)(2,1)S(1)} all-to-all(bf16[16,40,128]{2,1,0:T(8,128)(2,1)S(1)} %get-tuple-element.20), channel_id=1, replica_groups=mesh['groups'=2,'dap'=4,'sub'=4] {'dap','sub'}, dimensions={0} | all-to-all | bytes 327680 | tf_op jit(solution)/shard_map/all_to_all | solution.py:438
  17.9 0.0 copy-done
  18.0 0.0 copy-done.1
  18.0 0.0 copy-done.2
  18.0 0.0 copy-done.3
  18.0 1.6 %middle.1 = (bf16[256,384]{1,0:T(8,128)(2,1)S(1)}, bf16[256,128]{1,0:T(8,128)(2,1)S(1)}, bf16[256,128]{1,0:T(8,128)(2,1)S(1)}, f32[256,128]{1,0:T(8,128)S(1)}, f...) custom-call(bf16[16,40,128]{2,1,0:T(8,128)(2,1)S(1)} %all_to_all.10.recv_ref, ...), custom_call_target="tpu_custom_call" | custom-call | tf_op jit(solution)/shard_map/middle/pallas_call | solution.py:505
  19.6 0.0 collective-permute-start
  19.6 0.9 %cells.1 = (bf16[16,24,128]{2,1,0:T(8,128)(2,1)S(1)}, f32[64,128]{1,0:T(8,128)S(1)}) custom-call(bf16[256,384]{1,0:T(8,128)(2,1)S(1)} %get-tuple-element.21.dprojs_ref, bf16[256,128]{1,0:T(8,128)(2,1)S(1)} %get-tuple-element.22.x_ref, bf16[256,128]{1,0:T(8,128)(2,1)S(1)} %get-tuple-element.23.u_ref, f32[256,128]{1,0:T(8,128)S(1)} %get-tuple-element.24.gate_ref, ...), custom_call_target="tpu_custom_call" | custom-call | flops 41943040 | bytes 1310720 | tf_op jit(solution)/shard_map/cells/pallas_call | solution.py:526
  20.5 0.3 collective-permute-done.taken_ref
  20.9 12.1 %all_to_all.11.recv_ref = bf16[16,56,128]{2,1,0:T(8,128)(2,1)S(1)} all-to-all(bf16[16,56,128]{2,1,0:T(8,128)(2,1)S(1)} %pack.1), channel_id=1, replica_groups=mesh['groups'=2,'dap'=4,'sub'=4] {'dap','sub'}, dimensions={0} | all-to-all | bytes 458752 | tf_op jit(solution)/shard_map/all_to_all | solution.py:438
  33.0 0.1 collective-permute-start.1
  33.1 1.1 %after.1 = bf16[4,64,128]{2,1,0:T(8,128)(2,1)} custom-call(bf16[16,56,128]{2,1,0:T(8,128)(2,1)S(1)} %all_to_all.11.recv_ref, f32[256,128]{1,0:T(8,128)S(1)} %get-tuple-element.31.unit_ref, f32[256,1]{1,0:T(8,128)S(1)} %get-tuple-element.32.inverse_ref, f32[1,128]{1,0:T(1,128)S(1)} %get-tuple-element.33.gain_ref, ...), custom_call_target="tpu_custom_call" | custom-call | flops 655360 | bytes 655360 | tf_op jit(solution)/shard_map/after/pallas_call | solution.py:563
  34.2 0.1 collective-permute-done.1.theirs_ref
  34.3 0.6 %final.1 = (f32[64,128]{1,0:T(8,128)}, f32[64,128]{1,0:T(8,128)}) custom-call(f32[64,128]{1,0:T(8,128)S(1)} %adapters.1.mine_ref, f32[64,128]{1,0:T(8,128)S(1)} %collective-permute-done.1.theirs_ref), custom_call_target="tpu_custom_call" | custom-call | tf_op jit(solution)/shard_map/final/pallas_call | solution.py:579
  (2 shorter events, 0.0 us)
Async XLA Ops:
  2.1 15.8 %copy-start = (bf16[4,128,128]{2,1,0:T(8,128)(2,1)S(1)}, bf16[4,128,128]{2,1,0:T(8,128)(2,1)}, u32[]{:S(2)}) copy-start(bf16[4,128,128]{2,1,0:T(8,128)(2,1)} %weight_ref.3) | copy-start | bytes 393220
  2.2 15.8 %copy-start.1 = (bf16[4,128,16]{1,2,0:T(8,128)(2,1)S(1)}, bf16[4,128,16]{1,2,0:T(8,128)(2,1)}, u32[]{:S(2)}) copy-start(bf16[4,128,16]{1,2,0:T(8,128)(2,1)} %param.20) | copy-start | bytes 49156
  2.2 15.8 %copy-start.2 = (bf16[4,16,128]{2,1,0:T(8,128)(2,1)S(1)}, bf16[4,16,128]{2,1,0:T(8,128)(2,1)}, u32[]{:S(2)}) copy-start(bf16[4,16,128]{2,1,0:T(8,128)(2,1)} %up_ref.3) | copy-start | bytes 49156
  2.2 15.8 %copy-start.3 = (bf16[128,128]{1,0:T(8,128)(2,1)S(1)}, bf16[128,128]{1,0:T(8,128)(2,1)}, u32[]{:S(2)}) copy-start(bf16[128,128]{1,0:T(8,128)(2,1)} %out_weight_ref.1) | copy-start | bytes 98308
  19.6 1.2 %collective-permute-start = (f32[64,128]{1,0:T(8,128)S(1)}, f32[64,128]{1,0:T(8,128)S(1)}, u32[]{:S(2)}, u32[]{:S(2)}) collective-permute-start(f32[64,128]{1,0:T(8,128)S(1)} %get-tuple-element.30), channel_id=1, source_target_pairs={{0,1},{1,0},{2,3},{3,2},{4,5},{5,4},{6,7},{7,6},{8,9},{9,8},{10,11... | collective-permute-start | bytes 98312 | tf_op jit(solution)/shard_map/ppermute | solution.py:434
  33.0 1.3 %collective-permute-start.1 = (f32[64,128]{1,0:T(8,128)S(1)}, f32[64,128]{1,0:T(8,128)S(1)}, u32[]{:S(2)}, u32[]{:S(2)}) collective-permute-start(f32[64,128]{1,0:T(8,128)S(1)} %adapters.1.mine_ref), channel_id=1, source_target_pairs={{0,1},{1,0},{2,3},{3,2},{4,5},{5,4},{6,7},{7,6},{8,9},{9,8},{10,11... | collective-permute-start | bytes 98312 | tf_op jit(solution)/shard_map/ppermute | solution.py:434

commit v7 on v6

--- a/solution.py
+++ b/solution.py
@@ -210,16 +210,18 @@
     downs = stacked(down_ref, 3)
     ups = blocked(up_ref, 3)
 
+    spare = jnp.concatenate([ups[:, 2 * channels :], jnp.zeros_like(ups[:, :channels])], axis=1)
+
     def project(step):
         rows = pl.ds(pl.multiple_of(step * block, block), block)
         x = x_ref[rows]
         u = u_ref[rows]
-        update = nn(half(nt(x, downs)), ups)
-        pair01 = nn(x, beside(weight_ref, 0))
-        pair23 = nn(x, beside(weight_ref, 2))
-        q_ref[rows] = half(pair01[:, :channels] + update[:, :channels])
-        k_ref[rows] = half(pair01[:, channels:] + update[:, channels : 2 * channels])
-        v_ref[rows] = half(pair23[:, :channels] + update[:, 2 * channels :])
+        joined = jnp.concatenate([x, half(nt(x, downs))], axis=1)
+        pair01 = nn(joined, jnp.concatenate([beside(weight_ref, 0), ups[:, : 2 * channels]], axis=0))
+        pair23 = nn(joined, jnp.concatenate([beside(weight_ref, 2), spare], axis=0))
+        q_ref[rows] = half(pair01[:, :channels])
+        k_ref[rows] = half(pair01[:, channels:])
+        v_ref[rows] = half(pair23[:, :channels])
         gate = jax.nn.sigmoid(pair23[:, channels:])
         dgated = nt(u, out_weight_ref[...]) + nn(half(nt(u, up_ref[3])), down_ref[3])
         gate_ref[rows] = gate

time: 35.1 us -> 35.1 us (level)
  no operation moved by 1% of the time
where the time goes in v7:
time: 35.1 us; the launch traced here: 34.8 us
  blocking collectives  27.9 us (79%)
  Pallas kernels  5.71 us (16%)
  between operations  0.71 us (2%)
  waiting for transfers between devices  0.44 us (1%)
    all_to_all x2, blocking collectives, exchange(): lax.all_to_all(values, group_axes, split_axis=0, concat_axis=0, tiled=True)  27.9 us
    pallas_call x1, Pallas kernels, local(): pl.pallas_call(functools.partial(middle_kernel, own=own, heads=heads), ou...  1.56 us
    pallas_call x1, Pallas kernels, local(): pl.pallas_call(before_kernel, out_shape=(jax.ShapeDtypeStruct((peers, 2 *...  1.51 us
    pallas_call x1, Pallas kernels, local(): pl.pallas_call(after_kernel, out_shape=jax.ShapeDtypeStruct((own, count,...  1.08 us
    pallas_call x1, Pallas kernels, local(): pl.pallas_call(functools.partial(cells_kernel, own=own), out_shape=(jax.S...  0.89 us
  transfers between devices with their start and end apart: 2, of which 2 were waited for; matrix products, arithmetic and copies ran while one was open for 0% of the time, Pallas kernels for 6%

profile of v7, /device:TPU:0, one launch (start us, length us, event | category | flops | bytes accessed | tf_op | source)
XLA Modules:
  0.0 34.8 jit_solution(5326441741519086013)
XLA Ops:
  0.6 1.5 %before.1 = (bf16[16,40,128]{2,1,0:T(8,128)(2,1)S(1)}, f32[256,128]{1,0:T(8,128)S(1)}, f32[256,1]{1,0:T(8,128)S(1)}, f32[1,128]{1,0:T(1,128)S(1)}, bf16[4,128]{1,0:T(4,128)(2,1)S(1)}) custom-call(s32[64]{0:T(128)} %mask_hbm.1, s32[64]{0:T(128)} %label_hbm.1, s32[1,64]{1,0:T(1,128)} %bitcast.10, bf16[4,64,128]{2,1,0:T(8,128)(2,1)} %pair_hbm.1, ...), custom_call_target="tpu_custom_call" | custom-call | tf_op jit(solution)/shard_map/before/pallas_call | solution.py:472
  2.1 0.0 copy-start
  2.2 0.0 copy-start.1
  2.2 0.0 copy-start.2
  2.2 0.0 copy-start.3
  2.2 15.8 %all_to_all.10.recv_ref = bf16[16,40,128]{2,1,0:T(8,128)(2,1)S(1)} all-to-all(bf16[16,40,128]{2,1,0:T(8,128)(2,1)S(1)} %get-tuple-element.20), channel_id=1, replica_groups=mesh['groups'=2,'dap'=4,'sub'=4] {'dap','sub'}, dimensions={0} | all-to-all | bytes 327680 | tf_op jit(solution)/shard_map/all_to_all | solution.py:440
  17.9 0.0 copy-done
  18.0 0.0 copy-done.1
  18.0 0.0 copy-done.2
  18.0 0.0 copy-done.3
  18.0 1.6 %middle.1 = (bf16[256,384]{1,0:T(8,128)(2,1)S(1)}, bf16[256,128]{1,0:T(8,128)(2,1)S(1)}, bf16[256,128]{1,0:T(8,128)(2,1)S(1)}, f32[256,128]{1,0:T(8,128)S(1)}, f...) custom-call(bf16[16,40,128]{2,1,0:T(8,128)(2,1)S(1)} %all_to_all.10.recv_ref, ...), custom_call_target="tpu_custom_call" | custom-call | tf_op jit(solution)/shard_map/middle/pallas_call | solution.py:507
  19.5 0.0 collective-permute-start
  19.5 0.9 %cells.1 = (bf16[16,24,128]{2,1,0:T(8,128)(2,1)S(1)}, f32[64,128]{1,0:T(8,128)S(1)}) custom-call(bf16[256,384]{1,0:T(8,128)(2,1)S(1)} %get-tuple-element.21.dprojs_ref, bf16[256,128]{1,0:T(8,128)(2,1)S(1)} %get-tuple-element.22.x_ref, bf16[256,128]{1,0:T(8,128)(2,1)S(1)} %get-tuple-element.23.u_ref, f32[256,128]{1,0:T(8,128)S(1)} %get-tuple-element.24.gate_ref, ...), custom_call_target="tpu_custom_call" | custom-call | flops 41943040 | bytes 1310720 | tf_op jit(solution)/shard_map/cells/pallas_call | solution.py:528
  20.4 0.3 collective-permute-done.taken_ref
  20.8 12.1 %all_to_all.11.recv_ref = bf16[16,56,128]{2,1,0:T(8,128)(2,1)S(1)} all-to-all(bf16[16,56,128]{2,1,0:T(8,128)(2,1)S(1)} %pack.1), channel_id=1, replica_groups=mesh['groups'=2,'dap'=4,'sub'=4] {'dap','sub'}, dimensions={0} | all-to-all | bytes 458752 | tf_op jit(solution)/shard_map/all_to_all | solution.py:440
  32.9 0.1 collective-permute-start.1
  33.0 1.1 %after.1 = bf16[4,64,128]{2,1,0:T(8,128)(2,1)} custom-call(bf16[16,56,128]{2,1,0:T(8,128)(2,1)S(1)} %all_to_all.11.recv_ref, f32[256,128]{1,0:T(8,128)S(1)} %get-tuple-element.31.unit_ref, f32[256,1]{1,0:T(8,128)S(1)} %get-tuple-element.32.inverse_ref, f32[1,128]{1,0:T(1,128)S(1)} %get-tuple-element.33.gain_ref, ...), custom_call_target="tpu_custom_call" | custom-call | flops 655360 | bytes 655360 | tf_op jit(solution)/shard_map/after/pallas_call | solution.py:565
  34.1 0.1 collective-permute-done.1.theirs_ref
  34.2 0.6 %final.1 = (f32[64,128]{1,0:T(8,128)}, f32[64,128]{1,0:T(8,128)}) custom-call(f32[64,128]{1,0:T(8,128)S(1)} %adapters.1.mine_ref, f32[64,128]{1,0:T(8,128)S(1)} %collective-permute-done.1.theirs_ref), custom_call_target="tpu_custom_call" | custom-call | tf_op jit(solution)/shard_map/final/pallas_call | solution.py:581
  (2 shorter events, 0.0 us)
Async XLA Ops:
  2.1 15.8 %copy-start = (bf16[4,128,128]{2,1,0:T(8,128)(2,1)S(1)}, bf16[4,128,128]{2,1,0:T(8,128)(2,1)}, u32[]{:S(2)}) copy-start(bf16[4,128,128]{2,1,0:T(8,128)(2,1)} %weight_ref.3) | copy-start | bytes 393220
  2.2 15.8 %copy-start.1 = (bf16[4,128,16]{1,2,0:T(8,128)(2,1)S(1)}, bf16[4,128,16]{1,2,0:T(8,128)(2,1)}, u32[]{:S(2)}) copy-start(bf16[4,128,16]{1,2,0:T(8,128)(2,1)} %param.20) | copy-start | bytes 49156
  2.2 15.8 %copy-start.2 = (bf16[4,16,128]{2,1,0:T(8,128)(2,1)S(1)}, bf16[4,16,128]{2,1,0:T(8,128)(2,1)}, u32[]{:S(2)}) copy-start(bf16[4,16,128]{2,1,0:T(8,128)(2,1)} %up_ref.3) | copy-start | bytes 49156
  2.2 15.8 %copy-start.3 = (bf16[128,128]{1,0:T(8,128)(2,1)S(1)}, bf16[128,128]{1,0:T(8,128)(2,1)}, u32[]{:S(2)}) copy-start(bf16[128,128]{1,0:T(8,128)(2,1)} %out_weight_ref.1) | copy-start | bytes 98308
  19.5 1.2 %collective-permute-start = (f32[64,128]{1,0:T(8,128)S(1)}, f32[64,128]{1,0:T(8,128)S(1)}, u32[]{:S(2)}, u32[]{:S(2)}) collective-permute-start(f32[64,128]{1,0:T(8,128)S(1)} %get-tuple-element.30), channel_id=1, source_target_pairs={{0,1},{1,0},{2,3},{3,2},{4,5},{5,4},{6,7},{7,6},{8,9},{9,8},{10,11... | collective-permute-start | bytes 98312 | tf_op jit(solution)/shard_map/ppermute | solution.py:436
  32.9 1.3 %collective-permute-start.1 = (f32[64,128]{1,0:T(8,128)S(1)}, f32[64,128]{1,0:T(8,128)S(1)}, u32[]{:S(2)}, u32[]{:S(2)}) collective-permute-start(f32[64,128]{1,0:T(8,128)S(1)} %adapters.1.mine_ref), channel_id=1, source_target_pairs={{0,1},{1,0},{2,3},{3,2},{4,5},{5,4},{6,7},{7,6},{8,9},{9,8},{10,11... | collective-permute-start | bytes 98312 | tf_op jit(solution)/shard_map/ppermute | solution.py:436

commit v8 on v7

--- a/solution.py
+++ b/solution.py
@@ -249,7 +249,13 @@
             return jnp.concatenate([values * mark for mark in marks], axis=0)
 
         def collect(values):
-            return sum(values[head * joint : (head + 1) * joint] * spots[head] for head in range(joint_heads))
+            pieces = [values[head * joint : (head + 1) * joint] for head in range(joint_heads)]
+            if joint_heads < heads:
+                return sum(piece * spot for piece, spot in zip(pieces, spots))
+            found = pieces[-1]
+            for head in range(heads - 1):
+                found = jnp.where(head_of == head, pieces[head], found)
+            return found
 
         bias = bias_ref[:, pl.ds(column, block)]
         valid = bias > -1e38

time: 35.1 us -> 35.1 us (level)
  no operation moved by 1% of the time
where the time goes in v8:
time: 35.1 us; the launch traced here: 34.8 us
  blocking collectives  27.9 us (79%)
  Pallas kernels  5.71 us (16%)
  between operations  0.71 us (2%)
  waiting for transfers between devices  0.44 us (1%)
    all_to_all x2, blocking collectives, exchange(): lax.all_to_all(values, group_axes, split_axis=0, concat_axis=0, tiled=True)  27.9 us
    pallas_call x1, Pallas kernels, local(): pl.pallas_call(functools.partial(middle_kernel, own=own, heads=heads), ou...  1.56 us
    pallas_call x1, Pallas kernels, local(): pl.pallas_call(before_kernel, out_shape=(jax.ShapeDtypeStruct((peers, 2 *...  1.51 us
    pallas_call x1, Pallas kernels, local(): pl.pallas_call(after_kernel, out_shape=jax.ShapeDtypeStruct((own, count,...  1.08 us
    pallas_call x1, Pallas kernels, local(): pl.pallas_call(functools.partial(cells_kernel, own=own), out_shape=(jax.S...  0.89 us
  transfers between devices with their start and end apart: 2, of which 2 were waited for; matrix products, arithmetic and copies ran while one was open for 0% of the time, Pallas kernels for 6%

profile of v8, /device:TPU:0, one launch (start us, length us, event | category | flops | bytes accessed | tf_op | source)
XLA Modules:
  0.0 34.8 jit_solution(9764676138953416775)
XLA Ops:
  0.6 1.5 %before.1 = (bf16[16,40,128]{2,1,0:T(8,128)(2,1)S(1)}, f32[256,128]{1,0:T(8,128)S(1)}, f32[256,1]{1,0:T(8,128)S(1)}, f32[1,128]{1,0:T(1,128)S(1)}, bf16[4,128]{1,0:T(4,128)(2,1)S(1)}) custom-call(s32[64]{0:T(128)} %mask_hbm.1, s32[64]{0:T(128)} %label_hbm.1, s32[1,64]{1,0:T(1,128)} %bitcast.10, bf16[4,64,128]{2,1,0:T(8,128)(2,1)} %pair_hbm.1, ...), custom_call_target="tpu_custom_call" | custom-call | tf_op jit(solution)/shard_map/before/pallas_call | solution.py:478
  2.1 0.0 copy-start
  2.2 0.0 copy-start.1
  2.2 0.0 copy-start.2
  2.2 0.0 copy-start.3
  2.2 15.8 %all_to_all.10.recv_ref = bf16[16,40,128]{2,1,0:T(8,128)(2,1)S(1)} all-to-all(bf16[16,40,128]{2,1,0:T(8,128)(2,1)S(1)} %get-tuple-element.20), channel_id=1, replica_groups=mesh['groups'=2,'dap'=4,'sub'=4] {'dap','sub'}, dimensions={0} | all-to-all | bytes 327680 | tf_op jit(solution)/shard_map/all_to_all | solution.py:446
  17.9 0.0 copy-done
  18.0 0.0 copy-done.1
  18.0 0.0 copy-done.2
  18.0 0.0 copy-done.3
  18.0 1.6 %middle.1 = (bf16[256,384]{1,0:T(8,128)(2,1)S(1)}, bf16[256,128]{1,0:T(8,128)(2,1)S(1)}, bf16[256,128]{1,0:T(8,128)(2,1)S(1)}, f32[256,128]{1,0:T(8,128)S(1)}, f...) custom-call(bf16[16,40,128]{2,1,0:T(8,128)(2,1)S(1)} %all_to_all.10.recv_ref, ...), custom_call_target="tpu_custom_call" | custom-call | tf_op jit(solution)/shard_map/middle/pallas_call | solution.py:513
  19.5 0.0 collective-permute-start
  19.5 0.9 %cells.1 = (bf16[16,24,128]{2,1,0:T(8,128)(2,1)S(1)}, f32[64,128]{1,0:T(8,128)S(1)}) custom-call(bf16[256,384]{1,0:T(8,128)(2,1)S(1)} %get-tuple-element.21.dprojs_ref, bf16[256,128]{1,0:T(8,128)(2,1)S(1)} %get-tuple-element.22.x_ref, bf16[256,128]{1,0:T(8,128)(2,1)S(1)} %get-tuple-element.23.u_ref, f32[256,128]{1,0:T(8,128)S(1)} %get-tuple-element.24.gate_ref, ...), custom_call_target="tpu_custom_call" | custom-call | flops 41943040 | bytes 1310720 | tf_op jit(solution)/shard_map/cells/pallas_call | solution.py:534
  20.4 0.3 collective-permute-done.taken_ref
  20.8 12.1 %all_to_all.11.recv_ref = bf16[16,56,128]{2,1,0:T(8,128)(2,1)S(1)} all-to-all(bf16[16,56,128]{2,1,0:T(8,128)(2,1)S(1)} %pack.1), channel_id=1, replica_groups=mesh['groups'=2,'dap'=4,'sub'=4] {'dap','sub'}, dimensions={0} | all-to-all | bytes 458752 | tf_op jit(solution)/shard_map/all_to_all | solution.py:446
  32.9 0.1 collective-permute-start.1
  33.0 1.1 %after.1 = bf16[4,64,128]{2,1,0:T(8,128)(2,1)} custom-call(bf16[16,56,128]{2,1,0:T(8,128)(2,1)S(1)} %all_to_all.11.recv_ref, f32[256,128]{1,0:T(8,128)S(1)} %get-tuple-element.31.unit_ref, f32[256,1]{1,0:T(8,128)S(1)} %get-tuple-element.32.inverse_ref, f32[1,128]{1,0:T(1,128)S(1)} %get-tuple-element.33.gain_ref, ...), custom_call_target="tpu_custom_call" | custom-call | flops 655360 | bytes 655360 | tf_op jit(solution)/shard_map/after/pallas_call | solution.py:571
  34.1 0.1 collective-permute-done.1.theirs_ref
  34.2 0.6 %final.1 = (f32[64,128]{1,0:T(8,128)}, f32[64,128]{1,0:T(8,128)}) custom-call(f32[64,128]{1,0:T(8,128)S(1)} %adapters.1.mine_ref, f32[64,128]{1,0:T(8,128)S(1)} %collective-permute-done.1.theirs_ref), custom_call_target="tpu_custom_call" | custom-call | tf_op jit(solution)/shard_map/final/pallas_call | solution.py:587
  (2 shorter events, 0.0 us)
Async XLA Ops:
  2.1 15.8 %copy-start = (bf16[4,128,128]{2,1,0:T(8,128)(2,1)S(1)}, bf16[4,128,128]{2,1,0:T(8,128)(2,1)}, u32[]{:S(2)}) copy-start(bf16[4,128,128]{2,1,0:T(8,128)(2,1)} %weight_ref.3) | copy-start | bytes 393220
  2.2 15.8 %copy-start.1 = (bf16[4,128,16]{1,2,0:T(8,128)(2,1)S(1)}, bf16[4,128,16]{1,2,0:T(8,128)(2,1)}, u32[]{:S(2)}) copy-start(bf16[4,128,16]{1,2,0:T(8,128)(2,1)} %param.20) | copy-start | bytes 49156
  2.2 15.8 %copy-start.2 = (bf16[4,16,128]{2,1,0:T(8,128)(2,1)S(1)}, bf16[4,16,128]{2,1,0:T(8,128)(2,1)}, u32[]{:S(2)}) copy-start(bf16[4,16,128]{2,1,0:T(8,128)(2,1)} %up_ref.3) | copy-start | bytes 49156
  2.2 15.8 %copy-start.3 = (bf16[128,128]{1,0:T(8,128)(2,1)S(1)}, bf16[128,128]{1,0:T(8,128)(2,1)}, u32[]{:S(2)}) copy-start(bf16[128,128]{1,0:T(8,128)(2,1)} %out_weight_ref.1) | copy-start | bytes 98308
  19.5 1.2 %collective-permute-start = (f32[64,128]{1,0:T(8,128)S(1)}, f32[64,128]{1,0:T(8,128)S(1)}, u32[]{:S(2)}, u32[]{:S(2)}) collective-permute-start(f32[64,128]{1,0:T(8,128)S(1)} %get-tuple-element.30), channel_id=1, source_target_pairs={{0,1},{1,0},{2,3},{3,2},{4,5},{5,4},{6,7},{7,6},{8,9},{9,8},{10,11... | collective-permute-start | bytes 98312 | tf_op jit(solution)/shard_map/ppermute | solution.py:442
  32.9 1.3 %collective-permute-start.1 = (f32[64,128]{1,0:T(8,128)S(1)}, f32[64,128]{1,0:T(8,128)S(1)}, u32[]{:S(2)}, u32[]{:S(2)}) collective-permute-start(f32[64,128]{1,0:T(8,128)S(1)} %adapters.1.mine_ref), channel_id=1, source_target_pairs={{0,1},{1,0},{2,3},{3,2},{4,5},{5,4},{6,7},{7,6},{8,9},{9,8},{10,11... | collective-permute-start | bytes 98312 | tf_op jit(solution)/shard_map/ppermute | solution.py:442
